TPU v7x, 512 devices: a whole 4x8x8 slice. The times are simulated.
512 devices in a mesh: group: 8 (over x, core), dev: 64 (over z, y).
Axes of the slice: x: 4, y: 8, z: 8, core: 2. Of those that a mesh axis runs over, the one named last changes fastest.
Arguments:
- positions: float32 [3, 16777216], P(None, ('group', 'dev')), may hold values from -1 to 1
- strengths: float32 [3, 16777216], P(None, ('group', 'dev')), may hold values from -0.6 to 0.6
- active: int32 [131072], P(('group', 'dev')), may hold values from 0 to 1, as said below
- m2l_list: int32 [512, 3, 1152], P(('group', 'dev')), may hold values from -1 to 255, as said below
- p2p_list: int32 [512, 3, 128], P(('group', 'dev')), may hold values from -1 to 255, as said below
- local_pairs: int32 [512, 3, 128], P(('group', 'dev')), may hold values from -1 to 255, as said below
- m2l_ops: bfloat16 [32, 128, 128], replicated, may hold values from -3 to 3
Outputs:
- field: float32 [3, 16777216], P(None, ('group', 'dev'))
Inputs may be any that keep to these rules, and one draw needn't show every extreme that they name: Each device's 256 leaves hold between 4 and 32 active leaves; some device holds exactly 32. `m2l_list`: device (g, d), column b * 128 + c with b = 3 (i + 1) + (k + 1) for i, k in -1, 0, 1: row 0 is a leaf of device (g, d), row 1 an offset class below 32 equal to 8 - b modulo 9, row 2 an active leaf of device (g + i, d + k); or -1, 0, -1 in an empty column. Blocks towards positions outside the mesh are empty. Every active leaf is the target of exactly one slot of each offset class whose source position lies in the mesh. `p2p_list`: device (g, d), column j * 32 + c with (i, k) = (-1, -1), (-1, 0), (-1, 1), (0, -1) for j = 0, 1, 2, 3: rows 0 and 1 are active leaves of device (g, d) and of device (g + i, d + k), row 2 a neighbour class below 26; or -1, -1, 0 in an empty column. Blocks towards positions outside the mesh are empty. `local_pairs`: rows 0 and 1 are two different active leaves of the device, row 2 a neighbour class below 26; a device with k active leaves has live pairs in its first 4 k columns and -1, -1, 0 in the rest.
All inputs are finite; a program needn't handle non-finite values.
Results may differ from a plain program's by a relative error of at most 0.0013.
Values may be sent and summed in bfloat16 or wider, within the bound.
No kernel may reach another device: no remote copies, remote signals or barrier semaphores. Data moves between devices by JAX's collectives and lax.ppermute only.
A program may use at most 64 MiB of HBM per device.

v0:
```python
import math

import jax
import jax.numpy as jnp
from jax import lax
from jax.sharding import PartitionSpec as P

COEF = 128
ORDER = 5
OFFSETS = 32
ACT_MOST = 32


SMOOTH = 0.04
FORWARD_GROUP = (-1, -1, -1, 0)
FORWARD_MEMBER = (-1, 0, 1, -1)


def shifted_2(value, axis, steps):
    count = lax.axis_size(axis)
    first, last = (max(0, -steps), min(count, count - steps))
    return lax.ppermute(value, axis, [(source, source + steps) for source in range(first, last)])


def cheb_basis(coords, points, columns):
    angles = (2.0 * jnp.arange(points, dtype=jnp.float32) + 1.0) * (math.pi / (2.0 * points))
    degrees = jnp.arange(points, dtype=jnp.float32)
    table = jnp.cos(degrees[:, None] * angles[None, :])

    def one_dimension(values):
        previous = jnp.ones_like(values)
        current = values
        total = jnp.zeros(values.shape + (points,), jnp.float32) + 1.0 / points
        for degree in range(1, points):
            total = total + 2.0 / points * current[..., None] * table[degree]
            previous, current = (current, 2.0 * values * current - previous)
        return total

    along_x = one_dimension(coords[0])
    along_y = one_dimension(coords[1])
    along_z = one_dimension(coords[2])
    joint = along_x[..., :, None, None] * along_y[..., None, :, None] * along_z[..., None, None, :]
    joint = joint.reshape(coords.shape[1:] + (points**3,))
    padding = [(0, 0)] * (joint.ndim - 1) + [(0, columns - points**3)]
    return jnp.pad(joint, padding)


def multipoles(leaf_pos, leaf_str):
    count = leaf_pos.shape[1]
    width = math.gcd(count, 32)

    def multipoles_one_block(pieces):
        block_pos, block_str = pieces
        basis = cheb_basis(block_pos, ORDER, COEF)
        return jnp.einsum("clp,lpn->lcn", block_str, basis, precision=lax.Precision.HIGHEST)

    def regroup(array):
        return jnp.moveaxis(array.reshape((3, count // width, width) + array.shape[2:]), 1, 0)

    result = lax.map(multipoles_one_block, (regroup(leaf_pos), regroup(leaf_str)))
    return result.reshape(count, 3, COEF).astype(jnp.bfloat16)


def displacement(codes):
    shifted = codes + (codes >= 13).astype(jnp.int32)
    return jnp.stack([shifted // 9 - 1, shifted // 3 % 3 - 1, shifted % 3 - 1]).astype(jnp.float32)


def kernel_block(pos_left, pos_right, shift):
    pieces = [
        shift[component][:, None, None]
        + 0.5 * (pos_right[component][:, None, :] - pos_left[component][:, :, None])
        for component in range(3)
    ]
    return lax.rsqrt(pieces[0] * pieces[0] + pieces[1] * pieces[1] + pieces[2] * pieces[2] + SMOOTH)


def pair_terms(pos_left, str_left, pos_right, str_right, shift, want_right):
    count = pos_left.shape[1]
    block = math.gcd(count, 32)
    blocks = count // block

    def regroup(array):
        return jnp.moveaxis(array.reshape((array.shape[0], blocks, block) + array.shape[2:]), 1, 0)

    def pair_one_block(pieces):
        left_pos, left_str, right_pos, right_str, offset = pieces
        kernel = kernel_block(left_pos, right_pos, offset)
        results = []
        results.append(
            jnp.einsum("cpj,pij->cpi", right_str, kernel, precision=lax.Precision.HIGHEST)
        )
        if want_right:
            results.append(
                jnp.einsum("cpi,pij->cpj", left_str, kernel, precision=lax.Precision.HIGHEST)
            )
        return tuple(results)

    outputs = lax.map(
        pair_one_block,
        (
            regroup(pos_left),
            regroup(str_left),
            regroup(pos_right),
            regroup(str_right),
            regroup(shift),
        ),
    )
    return tuple(
        (
            jnp.moveaxis(piece_out, 0, 1).reshape((3, count) + piece_out.shape[3:])
            for piece_out in outputs
        )
    )


def compact(flags, most):
    leaf_count = flags.shape[0]
    ranking = jnp.cumsum(flags) - 1
    chosen = (ranking[None, :] == jnp.arange(most, dtype=jnp.int32)[:, None]) & (
        flags[None, :] == 1
    )
    active_index = jnp.sum(
        jnp.where(chosen, jnp.arange(leaf_count, dtype=jnp.int32)[None, :], 0), axis=1
    )
    active_live = jnp.any(chosen, axis=1).astype(jnp.float32)
    slot_of_leaf = jnp.where(flags == 1, ranking, most)
    return (active_index, active_live, slot_of_leaf)


def gather_leaves(leaf_pos, leaf_str, index):
    live = (index >= 0).astype(jnp.float32)
    safe = jnp.clip(index, 0, leaf_pos.shape[1] - 1).astype(jnp.int32)
    return (
        jnp.take(leaf_pos, safe, axis=1),
        jnp.take(leaf_str, safe, axis=1) * live[None, :, None],
    )


def leaf_slots(slot_of_leaf, leaves):
    return jnp.where(leaves >= 0, slot_of_leaf[jnp.maximum(leaves, 0)], ACT_MOST)


def add_to_slots(accum, slots, terms):
    picker = (jnp.arange(ACT_MOST, dtype=jnp.int32)[:, None] == slots[None, :]).astype(jnp.float32)
    return accum + jnp.einsum("an,cnp->cap", picker, terms, precision=lax.Precision.HIGHEST)


def on_device(positions, strengths, active, m2l_list, p2p_list, local_pairs, m2l_ops):
    leaf_count = active.shape[0]
    leaf_size = positions.shape[1] // leaf_count
    leaf_pos = positions.reshape(3, leaf_count, leaf_size)
    leaf_str = strengths.reshape(3, leaf_count, leaf_size)
    active_index, active_live, slot_of_leaf = compact(active, ACT_MOST)
    moments = multipoles(leaf_pos, leaf_str)
    groups = lax.axis_size("group")
    members = lax.axis_size("dev")
    my_group = lax.axis_index("group")
    my_member = lax.axis_index("dev")

    def arrived(step_group, step_member):
        sender_group = my_group - step_group
        sender_member = my_member - step_member
        return (
            (sender_group >= 0)
            & (sender_group < groups)
            & (sender_member >= 0)
            & (sender_member < members)
        )

    far_list = m2l_list[0]
    per_block = far_list.shape[1] // 9
    source_leaf = far_list[0].reshape(9, per_block)
    sent_moments = moments[jnp.maximum(source_leaf, 0)]
    sent_labels = jnp.stack(
        [far_list[2].reshape(9, per_block), far_list[1].reshape(9, per_block)], axis=1
    )
    got_moments = [sent_moments[4]] * 9
    got_labels = [sent_labels[4]] * 9
    for direction in range(9):
        if direction != 4:
            distance = (direction // 3 - 1) * members + direction % 3 - 1
            got_moments[direction], got_labels[direction] = shifted_2(
                (sent_moments[direction], sent_labels[direction]), ("group", "dev"), distance
            )
    inside = jnp.stack([arrived(direction // 3 - 1, direction % 3 - 1) for direction in range(9)])
    all_moments = jnp.stack(got_moments)
    all_labels = jnp.stack(got_labels)
    targets = jnp.where(inside[:, None], all_labels[:, 0], -1).reshape(-1)
    classes = all_labels[:, 1].reshape(-1)
    target_slot = leaf_slots(slot_of_leaf, targets)
    cell_key = target_slot * OFFSETS + classes
    offsets_total = m2l_ops.shape[0]
    coef_count = m2l_ops.shape[1]
    placer = (
        jnp.arange(ACT_MOST * offsets_total, dtype=jnp.int32)[:, None] == cell_key[None, :]
    ).astype(jnp.bfloat16)
    grid = jnp.dot(
        placer, all_moments.reshape(-1, 3 * coef_count), preferred_element_type=jnp.float32
    ).astype(jnp.bfloat16)
    grid = grid.reshape(ACT_MOST, offsets_total, 3, coef_count)
    local_exp = jnp.einsum("tock,okj->tcj", grid, m2l_ops, preferred_element_type=jnp.float32)
    active_pos = jnp.take(leaf_pos, active_index, axis=1)
    active_str = jnp.take(leaf_str, active_index, axis=1) * active_live[None, :, None]
    far_basis = cheb_basis(active_pos, ORDER, COEF)
    far_field = (
        jnp.einsum("tcn,tpn->ctp", local_exp, far_basis, precision=lax.Precision.HIGHEST)
        * active_live[None, :, None]
    )
    (self_field,) = pair_terms(
        active_pos, active_str, active_pos, active_str, jnp.zeros((3, ACT_MOST), jnp.float32), False
    )
    accum = self_field + far_field
    pair_list = local_pairs[0]
    first_pos, first_str = gather_leaves(leaf_pos, leaf_str, pair_list[0])
    second_pos, second_str = gather_leaves(leaf_pos, leaf_str, pair_list[1])
    to_first, to_second = pair_terms(
        first_pos, first_str, second_pos, second_str, displacement(pair_list[2]), True
    )
    accum = add_to_slots(accum, leaf_slots(slot_of_leaf, pair_list[0]), to_first)
    accum = add_to_slots(accum, leaf_slots(slot_of_leaf, pair_list[1]), to_second)
    near_list = p2p_list[0]
    per_side = near_list.shape[1] // 4
    for side in range(4):
        step_group = FORWARD_GROUP[side]
        step_member = FORWARD_MEMBER[side]
        distance = step_group * members + step_member
        mine = near_list[0, side * per_side : (side + 1) * per_side]
        theirs = near_list[1, side * per_side : (side + 1) * per_side]
        codes = near_list[2, side * per_side : (side + 1) * per_side]
        send_pos, send_str = gather_leaves(leaf_pos, leaf_str, mine)
        their_pos, their_str, their_labels = shifted_2(
            (send_pos, send_str, jnp.stack([theirs, codes])), ("group", "dev"), distance
        )
        own_leaf = jnp.where(arrived(step_group, step_member), their_labels[0], -1)
        own_pos, own_str = gather_leaves(leaf_pos, leaf_str, own_leaf)
        offsets = displacement(their_labels[1])
        to_them, to_own = pair_terms(their_pos, their_str, own_pos, own_str, offsets, True)
        returned = shifted_2(to_them, ("group", "dev"), -distance)
        accum = add_to_slots(accum, leaf_slots(slot_of_leaf, own_leaf), to_own)
        accum = add_to_slots(accum, leaf_slots(slot_of_leaf, mine), returned)
    placing = (
        (jnp.arange(leaf_count, dtype=jnp.int32)[:, None] == active_index[None, :])
        & (active_live[None, :] > 0)
    ).astype(jnp.float32)
    field = jnp.einsum("la,cap->clp", placing, accum, precision=lax.Precision.HIGHEST)
    return field.reshape(3, leaf_count * leaf_size)


def solution(mesh):
    in_specs = (
        P(None, ("group", "dev")),
        P(None, ("group", "dev")),
        P(("group", "dev")),
        P(("group", "dev"), None, None),
        P(("group", "dev"), None, None),
        P(("group", "dev"), None, None),
        P(),
    )
    out_specs = P(None, ("group", "dev"))
    return jax.shard_map(
        on_device, mesh=mesh, in_specs=in_specs, out_specs=out_specs, check_vma=False
    )
```

profile of v0, /device:TPU:4, one launch (start us, length us, event | category | flops | bytes accessed | tf_op | source)
XLA Modules:
  0.0 453.2 jit_solution(6127680723815279611)
XLA Ops:
  2.1 13.8 %collective-permute-start = (s32[2,128]{1,0:T(2,128)}, s32[2,128]{1,0:T(2,128)}, u32[]{:S(2)}, u32[]{:S(2)}) collective-permute-start(s32[2,128]{1,0:T(2,128)} %bitcast.54), channel_id=1, source_target_pairs={{65,0},{66,1},{67,2},{68,3},{69,4},{70,5},{71,6},{72,7},{73,8},{74... | collective-permute-start | bytes 3080 | tf_op jit(solution)/shard_map/ppermute | solution.py:22
  19.8 7.0 %collective-permute-start.3 = (s32[2,128]{1,0:T(2,128)}, s32[2,128]{1,0:T(2,128)}, u32[]{:S(2)}, u32[]{:S(2)}) collective-permute-start(s32[2,128]{1,0:T(2,128)} %bitcast.60), channel_id=1, source_target_pairs={{1,0},{2,1},{3,2},{4,3},{5,4},{6,5},{7,6},{8,7},{9,8},{10,9},{11,1... | collective-permute-start | bytes 3080 | tf_op jit(solution)/shard_map/ppermute | solution.py:22
  71.2 58.9 %while.8 = (s32[]{:T(128)}, bf16[8,32,3,128]{3,2,1,0:T(4,128)(2,1)S(1)}, f32[8,3,32,128]{3,1,2,0:T(4,128)}, f32[8,3,32,128]{3,2,0,1:T(8,128)}, s32[]{:T(128)}) while((s32[]{:T(128)}, bf16[8,32,3,128]{3,2,1,0:T(4,128)(2,1)S(1)}, f32[8,3,32,128]{3,1,2,0:T(4,128)}, f32[8,3,32,128]{3,2,0,1:T(8,128)}, s32[]{:T(128)}) %tuple.231), condition=%wide.region_5.7_spmd, body=%wide.region_4.6_spmd.sunk | while | flops 20115496 | bytes 10225085 | solution.py:60
  136.8 41.7 %while.18 = (s32[]{:T(128)}, f32[4,3,32,128]{3,1,2,0:T(4,128)}, f32[4,3,32,128]{3,1,2,0:T(4,128)}, f32[4,3,32]{2,0,1:T(4,128)S(1)}, f32[4,3,32,128]{3,2,0,1:T(8,...) while((s32[]{:T(128)}, f32[4,3,32,128]{3,1,2,0:T(4,128)}, ...), condition=%wide.region_7.10_spmd, body=%wide.region_6.9_spmd.sunk | while | flops 53477380 | bytes 858013 | solution.py:99
  141.4 5.8 %fusion.424 = f32[4,3,32,128]{3,1,2,0:T(4,128)} fusion(f32[4,3,32,128]{3,1,2,0:T(4,128)} %get-tuple-element.676, s32[]{:T(128)} %get-tuple-element.675, f32[32,128]{1,0:T(8,128)S(1)} %get-tuple-element.653, f32[32,128]{1,0:T(8,128)S(1)} %get-tuple-element.655, f32[32]{0:T(128)S(1)} %get-tuple-element.656, f32[32,128]{1,0:T(8,128)S(1)} %get-tuple-element.657, ...), kind=kOutput, calls=%fused_computation.91.clone.1 | convolution fusion | flops 26738688 | bytes 231936 | tf_op jit(solution)/shard_map/while/body/eval_jaxpr/cpj,pij->cpi/dot_general | solution.py:91
  151.8 5.8 %fusion.424 = f32[4,3,32,128]{3,1,2,0:T(4,128)} fusion(f32[4,3,32,128]{3,1,2,0:T(4,128)} %get-tuple-element.676, s32[]{:T(128)} %get-tuple-element.675, f32[32,128]{1,0:T(8,128)S(1)} %get-tuple-element.653, f32[32,128]{1,0:T(8,128)S(1)} %get-tuple-element.655, f32[32]{0:T(128)S(1)} %get-tuple-element.656, f32[32,128]{1,0:T(8,128)S(1)} %get-tuple-element.657, ...), kind=kOutput, calls=%fused_computation.91.clone.1 | convolution fusion | flops 26738688 | bytes 231936 | tf_op jit(solution)/shard_map/while/body/eval_jaxpr/cpj,pij->cpi/dot_general | solution.py:91
  162.3 5.8 %fusion.424 = f32[4,3,32,128]{3,1,2,0:T(4,128)} fusion(f32[4,3,32,128]{3,1,2,0:T(4,128)} %get-tuple-element.676, s32[]{:T(128)} %get-tuple-element.675, f32[32,128]{1,0:T(8,128)S(1)} %get-tuple-element.653, f32[32,128]{1,0:T(8,128)S(1)} %get-tuple-element.655, f32[32]{0:T(128)S(1)} %get-tuple-element.656, f32[32,128]{1,0:T(8,128)S(1)} %get-tuple-element.657, ...), kind=kOutput, calls=%fused_computation.91.clone.1 | convolution fusion | flops 26738688 | bytes 231936 | tf_op jit(solution)/shard_map/while/body/eval_jaxpr/cpj,pij->cpi/dot_general | solution.py:91
  172.7 5.8 %fusion.424 = f32[4,3,32,128]{3,1,2,0:T(4,128)} fusion(f32[4,3,32,128]{3,1,2,0:T(4,128)} %get-tuple-element.676, s32[]{:T(128)} %get-tuple-element.675, f32[32,128]{1,0:T(8,128)S(1)} %get-tuple-element.653, f32[32,128]{1,0:T(8,128)S(1)} %get-tuple-element.655, f32[32]{0:T(128)S(1)} %get-tuple-element.656, f32[32,128]{1,0:T(8,128)S(1)} %get-tuple-element.657, ...), kind=kOutput, calls=%fused_computation.91.clone.1 | convolution fusion | flops 26738688 | bytes 231936 | tf_op jit(solution)/shard_map/while/body/eval_jaxpr/cpj,pij->cpi/dot_general | solution.py:91
  185.8 5.8 %fusion.78 = f32[32,128,3]{1,2,0:T(4,128)} fusion(f32[32,128]{1,0:T(8,128)S(1)} %bitcast.655, f32[32,128]{1,0:T(8,128)S(1)} %bitcast.656, f32[32,128]{1,0:T(8,128)S(1)} %bitcast.654, f32[32,3,128]{2,1,0:T(4,128)S(1)} %copy-done.18, f32[32]{0:T(128)S(1)} %get-tuple-element.513, pred[32]{0:T(512)(128)(4,1)S(1)} %get-tuple-element.528), kind=kOutput, calls=%fused_computation.149 | convolution fusion | flops 25190400 | bytes 147616 | tf_op jit(solution)/shard_map/while/body/eval_jaxpr/cpj,pij->cpi/dot_general | solution.py:91
  204.5 5.2 %collective-permute-done.24 = s32[2,32]{1,0:T(2,128)S(1)} collective-permute-done((s32[2,32]{1,0:T(2,128)S(1)}, s32[2,32]{1,0:T(2,128)S(1)}, u32[]{:S(2)}, u32[]{:S(2)}) %collective-permute-start.24) | collective-permute-done | bytes 288 | tf_op jit(solution)/shard_map/ppermute | solution.py:22
  271.1 5.9 %collective-permute-start.5 = (s32[2,128]{1,0:T(2,128)}, s32[2,128]{1,0:T(2,128)S(1)}, u32[]{:S(2)}, u32[]{:S(2)}) collective-permute-start(s32[2,128]{1,0:T(2,128)} %bitcast.686), channel_id=1, source_target_pairs={{0,63},{1,64},{2,65},{3,66},{4,67},{5,68},{6,69},{7,70},{8,71},{9,... | collective-permute-start | bytes 3080 | tf_op jit(solution)/shard_map/ppermute | solution.py:22
  290.4 7.9 %collective-permute-start.18 = (f32[3,32,128]{2,0,1:T(4,128)}, f32[3,32,128]{2,0,1:T(4,128)}, u32[]{:S(2)}, u32[]{:S(2)}) collective-permute-start(f32[3,32,128]{2,0,1:T(4,128)} %bitcast_multiply_fusion.13), channel_id=1, source_target_pairs={{65,0},{66,1},{67,2},{68,3},{69,4},{70,5},{71,6},{72,7},{73,8},{74... | collective-permute-start | bytes 147464 | tf_op jit(solution)/shard_map/ppermute | solution.py:22
  311.2 7.3 %gather_fusion = s32[1152]{0:T(1024)S(1)} fusion(s32[256]{0:T(256)S(1)} %get-tuple-element.342, s32[2048]{0:T(1024)S(1)} %copy-done.24), kind=kCustom, calls=%fused_computation.22 | custom fusion | bytes 13824 | tf_op jit(solution)/shard_map/gather | solution.py:141
  321.7 5.3 %fusion.106 = f32[3,32,128]{2,0,1:T(4,128)S(1)} fusion(f32[32,128]{1,0:T(8,128)S(1)} %bitcast.677, f32[32,128]{1,0:T(8,128)S(1)} %bitcast.632, f32[32]{0:T(128)S(1)} %copy-done.80, f32[32,128]{1,0:T(8,128)S(1)} %bitcast.679, f32[32,128]{1,0:T(8,128)S(1)} %bitcast.634, f32[32]{0:T(128)S(1)} %copy-done.81, f32[32,128]{1,0:T(8,128)S(1)} %bitcast.675, ...), kind=kOutput, calls=%fused_computation.178 | convolution fusion | flops 26763264 | bytes 197152 | tf_op jit(solution)/shard_map/while/body/eval_jaxpr/cpj,pij->cpi/dot_general | solution.py:91
  327.0 6.1 %collective-permute-start.30 = (f32[3,32,128]{2,0,1:T(4,128)S(1)}, f32[3,32,128]{2,0,1:T(4,128)S(1)}, u32[]{:S(2)}, u32[]{:S(2)}) collective-permute-start(f32[3,32,128]{2,0,1:T(4,128)S(1)} %bitcast_multiply_fusion.4), channel_id=1, source_target_pairs={{1,0},{2,1},{3,2},{4,3},{5,4},{6,5},{7,6},{8,7},{9,8},{10,9},{11,1... | collective-permute-start | bytes 147464 | tf_op jit(solution)/shard_map/ppermute | solution.py:22
  334.4 5.3 %fusion.108 = f32[3,32,128]{2,0,1:T(4,128)S(1)} fusion(f32[32,128]{1,0:T(8,128)S(1)} %bitcast.671, f32[32,128]{1,0:T(8,128)S(1)} %bitcast.638, f32[32]{0:T(128)S(1)} %copy-done.83, f32[32,128]{1,0:T(8,128)S(1)} %bitcast.673, f32[32,128]{1,0:T(8,128)S(1)} %bitcast.640, f32[32]{0:T(128)S(1)} %copy-done.84, f32[32,128]{1,0:T(8,128)S(1)} %bitcast.669, ...), kind=kOutput, calls=%fused_computation.180 | convolution fusion | flops 26763264 | bytes 197152 | tf_op jit(solution)/shard_map/while/body/eval_jaxpr/cpj,pij->cpi/dot_general | solution.py:91
  342.3 5.3 %fusion.104 = f32[3,32,128]{2,0,1:T(4,128)S(1)} fusion(f32[32,128]{1,0:T(8,128)S(1)} %bitcast.665, f32[32,128]{1,0:T(8,128)S(1)} %bitcast.644, f32[32]{0:T(128)S(1)} %copy-done.86, f32[32,128]{1,0:T(8,128)S(1)} %bitcast.667, f32[32,128]{1,0:T(8,128)S(1)} %bitcast.646, f32[32]{0:T(128)S(1)} %copy-done.87, f32[32,128]{1,0:T(8,128)S(1)} %bitcast.663, ...), kind=kOutput, calls=%fused_computation.176 | convolution fusion | flops 26763264 | bytes 197152 | tf_op jit(solution)/shard_map/while/body/eval_jaxpr/cpj,pij->cpi/dot_general | solution.py:91
  349.7 5.3 %fusion.102 = f32[3,32,128]{2,0,1:T(4,128)S(1)} fusion(f32[32,128]{1,0:T(8,128)S(1)} %bitcast.659, f32[32,128]{1,0:T(8,128)S(1)} %bitcast.650, f32[32]{0:T(128)S(1)} %copy-done.89, f32[32,128]{1,0:T(8,128)S(1)} %bitcast.661, f32[32,128]{1,0:T(8,128)S(1)} %bitcast.652, f32[32]{0:T(128)S(1)} %copy-done.90, f32[32,128]{1,0:T(8,128)S(1)} %bitcast.657, ...), kind=kOutput, calls=%fused_computation.174 | convolution fusion | flops 26763264 | bytes 197152 | tf_op jit(solution)/shard_map/while/body/eval_jaxpr/cpj,pij->cpi/dot_general | solution.py:91
  368.2 5.2 %collective-permute-start.11 = (bf16[128,3,128]{2,1,0:T(4,128)(2,1)}, bf16[128,3,128]{2,1,0:T(4,128)(2,1)S(1)}, u32[]{:S(2)}, u32[]{:S(2)}) collective-permute-start(bf16[128,3,128]{2,1,0:T(4,128)(2,1)} %get-tuple-element.383), channel_id=1, source_target_pairs={{1,0},{2,1},{3,2},{4,3},{5,4},{6,5},{7,6},{8,7},{9,8},{10,9},{11,1... | collective-permute-start | bytes 294920 | tf_op jit(solution)/shard_map/ppermute | solution.py:22
  389.0 7.4 %collective-permute-done.19 = f32[3,32,128]{2,1,0:T(8,128)S(1)} collective-permute-done((f32[3,32,128]{2,1,0:T(8,128)S(1)}, f32[3,32,128]{2,1,0:T(8,128)S(1)}, u32[]{:S(2)}, u32[]{:S(2)}) %collective-permute-start.19) | collective-permute-done | bytes 49184 | tf_op jit(solution)/shard_map/ppermute | solution.py:22
  405.8 6.5 %collective-permute-done.31 = f32[3,32,128]{2,1,0:T(8,128)S(1)} collective-permute-done((f32[3,32,128]{2,1,0:T(8,128)S(1)}, f32[3,32,128]{2,1,0:T(8,128)S(1)}, u32[]{:S(2)}, u32[]{:S(2)}) %collective-permute-start.31) | collective-permute-done | bytes 49184 | tf_op jit(solution)/shard_map/ppermute | solution.py:22
  415.1 7.1 %collective-permute-start.13 = (bf16[128,3,128]{2,1,0:T(4,128)(2,1)S(1)}, bf16[128,3,128]{2,1,0:T(4,128)(2,1)S(1)}, u32[]{:S(2)}, u32[]{:S(2)}) collective-permute-start(bf16[128,3,128]{2,1,0:T(4,128)(2,1)S(1)} %copy-done.14), channel_id=1, source_target_pairs={{0,63},{1,64},{2,65},{3,66},{4,67},{5,68},{6,69},{7,70},{8,71},{9,... | collective-permute-start | bytes 294920 | tf_op jit(solution)/shard_map/ppermute | solution.py:22
  422.2 5.8 %collective-permute-start.14 = (bf16[128,3,128]{2,1,0:T(4,128)(2,1)S(1)}, bf16[128,3,128]{2,1,0:T(4,128)(2,1)S(1)}, u32[]{:S(2)}, u32[]{:S(2)}) collective-permute-start(bf16[128,3,128]{2,1,0:T(4,128)(2,1)S(1)} %copy-done.13), channel_id=1, source_target_pairs={{0,64},{1,65},{2,66},{3,67},{4,68},{5,69},{6,70},{7,71},{8,72},{9,... | collective-permute-start | bytes 294920 | tf_op jit(solution)/shard_map/ppermute | solution.py:22
  431.4 8.3 %collective-permute-done.15 = bf16[128,3,128]{2,1,0:T(4,128)(2,1)S(1)} collective-permute-done((bf16[128,3,128]{2,1,0:T(4,128)(2,1)S(1)}, bf16[128,3,128]{2,1,0:T(4,128)(2,1)S(1)}, u32[]{:S(2)}, u32[]{:S(2)}) %collective-permute-start.15) | collective-permute-done | bytes 98336 | tf_op jit(solution)/shard_map/ppermute | solution.py:22
  (540 shorter events, 306.9 us)
Async XLA Ops:
  2.1 269.0 %collective-permute-start = (s32[2,128]{1,0:T(2,128)}, s32[2,128]{1,0:T(2,128)}, u32[]{:S(2)}, u32[]{:S(2)}) collective-permute-start(s32[2,128]{1,0:T(2,128)} %bitcast.54), channel_id=1, source_target_pairs={{65,0},{66,1},{67,2},{68,3},{69,4},{70,5},{71,6},{72,7},{73,8},{74... | collective-permute-start | bytes 3080 | tf_op jit(solution)/shard_map/ppermute | solution.py:22
  15.9 261.8 %collective-permute-start.1 = (s32[2,128]{1,0:T(2,128)}, s32[2,128]{1,0:T(2,128)}, u32[]{:S(2)}, u32[]{:S(2)}) collective-permute-start(s32[2,128]{1,0:T(2,128)} %bitcast.56), channel_id=1, source_target_pairs={{64,0},{65,1},{66,2},{67,3},{68,4},{69,5},{70,6},{71,7},{72,8},{73... | collective-permute-start | bytes 3080 | tf_op jit(solution)/shard_map/ppermute | solution.py:22
  17.9 263.0 %collective-permute-start.2 = (s32[2,128]{1,0:T(2,128)}, s32[2,128]{1,0:T(2,128)}, u32[]{:S(2)}, u32[]{:S(2)}) collective-permute-start(s32[2,128]{1,0:T(2,128)} %bitcast.58), channel_id=1, source_target_pairs={{63,0},{64,1},{65,2},{66,3},{67,4},{68,5},{69,6},{70,7},{71,8},{72... | collective-permute-start | bytes 3080 | tf_op jit(solution)/shard_map/ppermute | solution.py:22
  19.8 263.6 %collective-permute-start.3 = (s32[2,128]{1,0:T(2,128)}, s32[2,128]{1,0:T(2,128)}, u32[]{:S(2)}, u32[]{:S(2)}) collective-permute-start(s32[2,128]{1,0:T(2,128)} %bitcast.60), channel_id=1, source_target_pairs={{1,0},{2,1},{3,2},{4,3},{5,4},{6,5},{7,6},{8,7},{9,8},{10,9},{11,1... | collective-permute-start | bytes 3080 | tf_op jit(solution)/shard_map/ppermute | solution.py:22
  28.2 167.9 %collective-permute-start.20 = (s32[2,32]{1,0:T(2,128)}, s32[2,32]{1,0:T(2,128)}, u32[]{:S(2)}, u32[]{:S(2)}) collective-permute-start(s32[2,32]{1,0:T(2,128)} %get-tuple-element.464), channel_id=1, source_target_pairs={{64,0},{65,1},{66,2},{67,3},{68,4},{69,5},{70,6},{71,7},{72,8},{73... | collective-permute-start | bytes 776 | tf_op jit(solution)/shard_map/ppermute | solution.py:22
  209.7 12.7 %collective-permute-start.28 = (s32[2,32]{1,0:T(2,128)}, s32[2,32]{1,0:T(2,128)}, u32[]{:S(2)}, u32[]{:S(2)}) collective-permute-start(s32[2,32]{1,0:T(2,128)} %get-tuple-element.462), channel_id=1, source_target_pairs={{1,0},{2,1},{3,2},{4,3},{5,4},{6,5},{7,6},{8,7},{9,8},{10,9},{11,1... | collective-permute-start | bytes 776 | tf_op jit(solution)/shard_map/ppermute | solution.py:22
  222.4 65.4 %collective-permute-start.4 = (s32[2,128]{1,0:T(2,128)}, s32[2,128]{1,0:T(2,128)}, u32[]{:S(2)}, u32[]{:S(2)}) collective-permute-start(s32[2,128]{1,0:T(2,128)} %bitcast.687), channel_id=1, source_target_pairs={{0,1},{1,2},{2,3},{3,4},{4,5},{5,6},{6,7},{7,8},{8,9},{9,10},{10,1... | collective-permute-start | bytes 3080 | tf_op jit(solution)/shard_map/ppermute | solution.py:22
  271.1 19.2 %collective-permute-start.5 = (s32[2,128]{1,0:T(2,128)}, s32[2,128]{1,0:T(2,128)S(1)}, u32[]{:S(2)}, u32[]{:S(2)}) collective-permute-start(s32[2,128]{1,0:T(2,128)} %bitcast.686), channel_id=1, source_target_pairs={{0,63},{1,64},{2,65},{3,66},{4,67},{5,68},{6,69},{7,70},{8,71},{9,... | collective-permute-start | bytes 3080 | tf_op jit(solution)/shard_map/ppermute | solution.py:22
  277.8 20.5 %collective-permute-start.6 = (s32[2,128]{1,0:T(2,128)}, s32[2,128]{1,0:T(2,128)S(1)}, u32[]{:S(2)}, u32[]{:S(2)}) collective-permute-start(s32[2,128]{1,0:T(2,128)} %bitcast.685), channel_id=1, source_target_pairs={{0,64},{1,65},{2,66},{3,67},{4,68},{5,69},{6,70},{7,71},{8,72},{9,... | collective-permute-start | bytes 3080 | tf_op jit(solution)/shard_map/ppermute | solution.py:22
  280.8 19.4 %collective-permute-start.7 = (s32[2,128]{1,0:T(2,128)}, s32[2,128]{1,0:T(2,128)S(1)}, u32[]{:S(2)}, u32[]{:S(2)}) collective-permute-start(s32[2,128]{1,0:T(2,128)} %bitcast.684), channel_id=1, source_target_pairs={{0,65},{1,66},{2,67},{3,68},{4,69},{5,70},{6,71},{7,72},{8,73},{9,... | collective-permute-start | bytes 3080 | tf_op jit(solution)/shard_map/ppermute | solution.py:22
  283.4 35.2 %collective-permute-start.21 = (f32[3,32,128]{2,0,1:T(4,128)}, f32[3,32,128]{2,0,1:T(4,128)}, u32[]{:S(2)}, u32[]{:S(2)}) collective-permute-start(f32[3,32,128]{2,0,1:T(4,128)} %select_bitcast_fusion.6), channel_id=1, source_target_pairs={{64,0},{65,1},{66,2},{67,3},{68,4},{69,5},{70,6},{71,7},{72,8},{73... | collective-permute-start | bytes 147464 | tf_op jit(solution)/shard_map/ppermute | solution.py:22
  287.8 67.2 %collective-permute-start.22 = (f32[3,32,128]{2,0,1:T(4,128)}, f32[3,32,128]{2,0,1:T(4,128)}, u32[]{:S(2)}, u32[]{:S(2)}) collective-permute-start(f32[3,32,128]{2,0,1:T(4,128)} %bitcast_multiply_fusion.10), channel_id=1, source_target_pairs={{64,0},{65,1},{66,2},{67,3},{68,4},{69,5},{70,6},{71,7},{72,8},{73... | collective-permute-start | bytes 147464 | tf_op jit(solution)/shard_map/ppermute | solution.py:22
  290.4 71.2 %collective-permute-start.18 = (f32[3,32,128]{2,0,1:T(4,128)}, f32[3,32,128]{2,0,1:T(4,128)}, u32[]{:S(2)}, u32[]{:S(2)}) collective-permute-start(f32[3,32,128]{2,0,1:T(4,128)} %bitcast_multiply_fusion.13), channel_id=1, source_target_pairs={{65,0},{66,1},{67,2},{68,3},{69,4},{70,5},{71,6},{72,7},{73,8},{74... | collective-permute-start | bytes 147464 | tf_op jit(solution)/shard_map/ppermute | solution.py:22
  298.3 28.8 %collective-permute-start.17 = (f32[3,32,128]{2,0,1:T(4,128)}, f32[3,32,128]{2,0,1:T(4,128)}, u32[]{:S(2)}, u32[]{:S(2)}) collective-permute-start(f32[3,32,128]{2,0,1:T(4,128)} %select_bitcast_fusion.8), channel_id=1, source_target_pairs={{65,0},{66,1},{67,2},{68,3},{69,4},{70,5},{71,6},{72,7},{73,8},{74... | collective-permute-start | bytes 147464 | tf_op jit(solution)/shard_map/ppermute | solution.py:22
  300.2 67.9 %collective-permute-start.26 = (f32[3,32,128]{2,0,1:T(4,128)}, f32[3,32,128]{2,0,1:T(4,128)}, u32[]{:S(2)}, u32[]{:S(2)}) collective-permute-start(f32[3,32,128]{2,0,1:T(4,128)} %bitcast_multiply_fusion.7), channel_id=1, source_target_pairs={{63,0},{64,1},{65,2},{66,3},{67,4},{68,5},{69,6},{70,7},{71,8},{72... | collective-permute-start | bytes 147464 | tf_op jit(solution)/shard_map/ppermute | solution.py:22
  318.6 21.1 %collective-permute-start.25 = (f32[3,32,128]{2,0,1:T(4,128)S(1)}, f32[3,32,128]{2,0,1:T(4,128)S(1)}, u32[]{:S(2)}, u32[]{:S(2)}) collective-permute-start(f32[3,32,128]{2,0,1:T(4,128)S(1)} %copy-done.17), channel_id=1, source_target_pairs={{63,0},{64,1},{65,2},{66,3},{67,4},{68,5},{69,6},{70,7},{71,8},{72... | collective-permute-start | bytes 147464 | tf_op jit(solution)/shard_map/ppermute | solution.py:22
  327.0 50.9 %collective-permute-start.30 = (f32[3,32,128]{2,0,1:T(4,128)S(1)}, f32[3,32,128]{2,0,1:T(4,128)S(1)}, u32[]{:S(2)}, u32[]{:S(2)}) collective-permute-start(f32[3,32,128]{2,0,1:T(4,128)S(1)} %bitcast_multiply_fusion.4), channel_id=1, source_target_pairs={{1,0},{2,1},{3,2},{4,3},{5,4},{6,5},{7,6},{8,7},{9,8},{10,9},{11,1... | collective-permute-start | bytes 147464 | tf_op jit(solution)/shard_map/ppermute | solution.py:22
  347.6 67.4 %collective-permute-start.8 = (bf16[128,3,128]{2,1,0:T(4,128)(2,1)}, bf16[128,3,128]{2,1,0:T(4,128)(2,1)S(1)}, u32[]{:S(2)}, u32[]{:S(2)}) collective-permute-start(bf16[128,3,128]{2,1,0:T(4,128)(2,1)} %get-tuple-element.386), channel_id=1, source_target_pairs={{65,0},{66,1},{67,2},{68,3},{69,4},{70,5},{71,6},{72,7},{73,8},{74... | collective-permute-start | bytes 294920 | tf_op jit(solution)/shard_map/ppermute | solution.py:22
  355.0 67.2 %collective-permute-start.9 = (bf16[128,3,128]{2,1,0:T(4,128)(2,1)}, bf16[128,3,128]{2,1,0:T(4,128)(2,1)S(1)}, u32[]{:S(2)}, u32[]{:S(2)}) collective-permute-start(bf16[128,3,128]{2,1,0:T(4,128)(2,1)} %get-tuple-element.385), channel_id=1, source_target_pairs={{64,0},{65,1},{66,2},{67,3},{68,4},{69,5},{70,6},{71,7},{72,8},{73... | collective-permute-start | bytes 294920 | tf_op jit(solution)/shard_map/ppermute | solution.py:22
  361.6 66.5 %collective-permute-start.10 = (bf16[128,3,128]{2,1,0:T(4,128)(2,1)}, bf16[128,3,128]{2,1,0:T(4,128)(2,1)S(1)}, u32[]{:S(2)}, u32[]{:S(2)}) collective-permute-start(bf16[128,3,128]{2,1,0:T(4,128)(2,1)} %get-tuple-element.384), channel_id=1, source_target_pairs={{63,0},{64,1},{65,2},{66,3},{67,4},{68,5},{69,6},{70,7},{71,8},{72... | collective-permute-start | bytes 294920 | tf_op jit(solution)/shard_map/ppermute | solution.py:22
  368.2 61.9 %collective-permute-start.11 = (bf16[128,3,128]{2,1,0:T(4,128)(2,1)}, bf16[128,3,128]{2,1,0:T(4,128)(2,1)S(1)}, u32[]{:S(2)}, u32[]{:S(2)}) collective-permute-start(bf16[128,3,128]{2,1,0:T(4,128)(2,1)} %get-tuple-element.383), channel_id=1, source_target_pairs={{1,0},{2,1},{3,2},{4,3},{5,4},{6,5},{7,6},{8,7},{9,8},{10,9},{11,1... | collective-permute-start | bytes 294920 | tf_op jit(solution)/shard_map/ppermute | solution.py:22
  412.4 18.8 %collective-permute-start.12 = (bf16[128,3,128]{2,1,0:T(4,128)(2,1)S(1)}, bf16[128,3,128]{2,1,0:T(4,128)(2,1)S(1)}, u32[]{:S(2)}, u32[]{:S(2)}) collective-permute-start(bf16[128,3,128]{2,1,0:T(4,128)(2,1)S(1)} %copy-done.15), channel_id=1, source_target_pairs={{0,1},{1,2},{2,3},{3,4},{4,5},{5,6},{6,7},{7,8},{8,9},{9,10},{10,1... | collective-permute-start | bytes 294920 | tf_op jit(solution)/shard_map/ppermute | solution.py:22
  415.1 16.1 %collective-permute-start.13 = (bf16[128,3,128]{2,1,0:T(4,128)(2,1)S(1)}, bf16[128,3,128]{2,1,0:T(4,128)(2,1)S(1)}, u32[]{:S(2)}, u32[]{:S(2)}) collective-permute-start(bf16[128,3,128]{2,1,0:T(4,128)(2,1)S(1)} %copy-done.14), channel_id=1, source_target_pairs={{0,63},{1,64},{2,65},{3,66},{4,67},{5,68},{6,69},{7,70},{8,71},{9,... | collective-permute-start | bytes 294920 | tf_op jit(solution)/shard_map/ppermute | solution.py:22
  428.1 11.5 %collective-permute-start.15 = (bf16[128,3,128]{2,1,0:T(4,128)(2,1)S(1)}, bf16[128,3,128]{2,1,0:T(4,128)(2,1)S(1)}, u32[]{:S(2)}, u32[]{:S(2)}) collective-permute-start(bf16[128,3,128]{2,1,0:T(4,128)(2,1)S(1)} %copy-done.12), channel_id=1, source_target_pairs={{0,65},{1,66},{2,67},{3,68},{4,69},{5,70},{6,71},{7,72},{8,73},{9,... | collective-permute-start | bytes 294920 | tf_op jit(solution)/shard_map/ppermute | solution.py:22
  (107 other events, 1624.7 us)
where the time goes:
time: 457 us; the launch traced here: 453 us
  matrix products  121 us (26%)
  local copies, waits for them, and re-layouts  117 us (26%)
  starting transfers between devices  117 us (26%)
  other arithmetic  66.7 us (15%)
  waiting for transfers between devices  29.6 us (6%)
    ppermute x32, starting transfers between devices, shifted_2(): lax.ppermute(value, axis, [(source, source + steps) for source in range(f...  117 us
    dot_general x9, matrix products, pair_one_block(): jnp.einsum('cpj,pij->cpi', right_str, kernel, precision=lax.Precision.HIG...  50.4 us
    dot_general x8, matrix products, pair_one_block(): jnp.einsum('cpi,pij->cpj', left_str, kernel, precision=lax.Precision.HIGH...  34.8 us
    ppermute x32, waiting for transfers between devices, shifted_2(): lax.ppermute(value, axis, [(source, source + steps) for source in range(f...  29.6 us
    gather x10, local copies, waits for them, and re-layouts, gather_leaves(): jnp.take(leaf_str, safe, axis=1) * live[None, :, None]  22.3 us
    dot_general x8, matrix products, multipoles_one_block(): jnp.einsum('clp,lpn->lcn', block_str, basis, precision=lax.Precision.HIGH...  21.2 us
    gather x10, local copies, waits for them, and re-layouts, gather_leaves(): jnp.take(leaf_pos, safe, axis=1)  19.9 us
    mul x9, local copies, waits for them, and re-layouts, cheb_basis(): along_x[..., :, None, None] * along_y[..., None, :, None]  18.3 us
  transfers between devices with their start and end apart: 32, of which 6 were waited for; matrix products, arithmetic and copies ran while one was open for 64% of the time, Pallas kernels for 0%

commit v1 on v0

v1 whole, which is shorter than its diff:
```python
import math

import jax
import jax.numpy as jnp
import ml_dtypes
import numpy as np
from jax import lax
from jax.experimental import pallas as pl
from jax.experimental.pallas import tpu as pltpu
from jax.sharding import PartitionSpec as P

COEF = 128
ORDER = 5
OFFSETS = 32
ACT_MOST = 32
LEAF_PART = 128
LEAF_DEV = 256
PCAP = 32
DEAD = ACT_MOST
ROWS_LEAF = 6
META = ROWS_LEAF * ACT_MOST
PACKET = META + 8
GROUP_LEAVES = 8
PAIRS = 16
FIRST = 4
SMOOTH = 0.04
FORWARD_GROUP = (-1, -1, -1, 0)
FORWARD_MEMBER = (-1, 0, 1, -1)
VMEM_LIMIT = 40 * 1024 * 1024

F32 = jnp.float32
BF16 = jnp.bfloat16
NT = (((1,), (1,)), ((), ()))
NN = (((1,), (0,)), ((), ()))


def dot(left, right, dims=NN):
    return lax.dot_general(left, right, dims, preferred_element_type=F32)


def split(value):
    high = value.astype(BF16)
    return high, (value - high.astype(F32)).astype(BF16)


def iota(shape, dim):
    return lax.broadcasted_iota(jnp.int32, shape, dim)


def combination(rows):
    table = np.zeros((len(rows), 32), np.float64)
    for at, row in enumerate(rows):
        if row is None:
            continue
        raw, point = row
        if point is None:
            table[at, raw] = 1.0
            continue
        table[at, 6] = 1.0 / ORDER
        for degree in range(1, ORDER):
            angle = degree * (2 * point + 1) * math.pi / (2 * ORDER)
            table[at, 8 * (degree - 1) + raw] = 2.0 / ORDER * math.cos(angle)
    high = table.astype(ml_dtypes.bfloat16)
    low = (table - high.astype(np.float64)).astype(ml_dtypes.bfloat16)
    return np.concatenate([high, high, low], axis=1)


def moment_rows():
    points = range(ORDER)
    along_x = [(0, a) for c in range(3) for a in points] + [None]
    strength = [(3 + c, None) for c in range(3) for a in points] + [None]
    along_y = [(1, b) for b in points for g in points] + [None] * 7
    along_z = [(2, g) for b in points for g in points] + [None] * 7
    return combination(along_x + strength + along_y + along_z)


def basis_rows():
    points = range(ORDER)
    every = [(a, b, g) for a in points for b in points for g in points]
    return combination(
        [(dim, n[dim]) if n is not None else None for dim in range(3) for n in every + [None] * 3]
    )


def spreading():
    table = np.zeros((ORDER, 32, COEF), np.float32)
    for a in range(ORDER):
        for bg in range(ORDER**2):
            table[a, bg, a * ORDER**2 + bg] = 1.0
    return table.astype(ml_dtypes.bfloat16)


def displacements():
    table = np.zeros((2, 32, 8, LEAF_PART), np.float32)
    for code in range(26):
        shifted = code + (1 if code >= 13 else 0)
        vector = (shifted // 9 - 1, shifted // 3 % 3 - 1, shifted % 3 - 1)
        for dim in range(3):
            table[0, code, dim] = vector[dim]
            table[1, code, dim] = -vector[dim]
    return table.reshape(64, 8, LEAF_PART)


def features(raw):
    second = 2.0 * raw * raw - 1.0
    third = 2.0 * raw * second - raw
    fourth = 2.0 * raw * third - second
    high, low = split(jnp.concatenate([raw, second, third, fourth], axis=0))
    return jnp.concatenate([high, low, high], axis=0)


def presence(targets, classes, residue):
    leaves = iota((LEAF_DEV, 128), 0)
    hit = (leaves == targets).astype(F32).astype(BF16)
    counted = jnp.broadcast_to((classes == residue) & (targets >= 0), (16, 128))
    return dot(counted.astype(F32).astype(BF16), hit, NT).astype(BF16)


def below(targets):
    return (iota((LEAF_DEV, 128), 0) < targets).astype(F32).astype(BF16)


def pack_kernel(
    flags_ref, pos_ref, str_ref, active_ref, far_ref, near_ref, local_ref, packet_ref, lists_ref, index_ref
):
    def enter(leaf, count):
        index_ref[count] = leaf
        return count + flags_ref[leaf]

    for slot in range(ACT_MOST):
        index_ref[slot] = 0
    count = lax.fori_loop(0, LEAF_DEV, enter, 0, unroll=8)
    index_ref[ACT_MOST] = count
    for slot in range(ACT_MOST):
        leaf = index_ref[slot]
        leaf = jnp.where(slot < count, leaf, 0)
        here = pl.ds(pl.multiple_of(leaf * LEAF_PART, LEAF_PART), LEAF_PART)
        packet_ref[ROWS_LEAF * slot : ROWS_LEAF * slot + 3, :] = pos_ref[:, here]
        packet_ref[ROWS_LEAF * slot + 3 : ROWS_LEAF * slot + 6, :] = str_ref[:, here]

    own = jnp.broadcast_to(active_ref[...].astype(F32), (16, LEAF_DEV)).astype(BF16)

    def own_slot(row):
        rank = dot(own, below(row))[0:1]
        return jnp.where(row >= 0, rank.astype(jnp.int32), DEAD)

    second = near_ref[1:2, :]
    under = below(second)
    lanes = iota((1, 128), 1)
    second_slot = jnp.full((1, 128), DEAD, jnp.int32)
    for side in range(4):
        direction = 3 * (FORWARD_GROUP[side] + 1) + FORWARD_MEMBER[side] + 1
        there = presence(far_ref[18 + direction : 19 + direction, :], far_ref[9 + direction : 10 + direction, :], 8 - direction)
        rank = dot(there, under)[0:1].astype(jnp.int32)
        mine = (lanes >= side * PCAP) & (lanes < (side + 1) * PCAP) & (second >= 0)
        second_slot = jnp.where(mine, rank, second_slot)
    first_slot = own_slot(near_ref[0:1, :])
    codes = near_ref[2:3, :]
    lists_ref[0:1, :] = own_slot(local_ref[0:1, :])
    lists_ref[1:2, :] = own_slot(local_ref[1:2, :])
    lists_ref[2:3, :] = local_ref[2:3, :]
    lists_ref[3:4, :] = first_slot
    lists_ref[4:5, :] = second_slot
    lists_ref[5:6, :] = codes
    lists_ref[6:8, :] = jnp.zeros((2, 128), jnp.int32)
    packet_ref[META : META + 1, :] = first_slot.astype(F32)
    packet_ref[META + 1 : META + 2, :] = second_slot.astype(F32)
    packet_ref[META + 2 : META + 3, :] = codes.astype(F32)
    packet_ref[META + 3 :, :] = jnp.zeros((5, 128), F32)


def far_kernel(
    pos_ref, str_ref, far_ref, ops_ref, mix_ref, spread_ref, *rest
):
    outs, (cell_ref, moment_ref, pick_ref, place_ref, got_ref) = rest[:3], rest[3:]
    empty = jnp.zeros((7, 128), jnp.int32)
    classes = far_ref[9:18, :]
    targets = far_ref[18:27, :]
    residues = 8 - iota((9, 128), 0)
    counted = jnp.where((classes == residues) & (targets >= 0), targets, LEAF_DEV)
    counted = jnp.concatenate([counted, empty], axis=0).astype(F32).T
    sources = jnp.concatenate([far_ref[0:9, :], empty], axis=0).astype(F32).T
    leaves = iota((128, LEAF_DEV), 1).astype(F32)
    for direction in range(9):
        target = targets[direction : direction + 1]
        less = counted[:, direction : direction + 1] < target.astype(F32)
        rank = jnp.sum(jnp.where(less, 1.0, 0.0), axis=0, keepdims=True).astype(jnp.int32)
        kind = classes[direction : direction + 1]
        step = (kind >= 9).astype(jnp.int32) + (kind >= 18).astype(jnp.int32) + (kind >= 27).astype(jnp.int32)
        key = jnp.where(target >= 0, step * ACT_MOST + rank, -1)
        rows = slice(direction * 128, (direction + 1) * 128)
        place_ref[rows, :] = (iota((128, 128), 0) == key).astype(F32).astype(BF16)
        pick_ref[rows, :] = (sources[:, direction : direction + 1] == leaves).astype(F32).astype(BF16)

    mix = mix_ref[...]
    width = GROUP_LEAVES * LEAF_PART
    lane_leaf = iota((32, 128), 1) // 16

    def parts(value):
        return [value[:, leaf * LEAF_PART : (leaf + 1) * LEAF_PART] for leaf in range(GROUP_LEAVES)]

    def expand(block, carry):
        here = pl.ds(pl.multiple_of(block * width, width), width)
        raw = jnp.concatenate(
            [pos_ref[:, here], str_ref[:, here], jnp.ones((1, width), F32), jnp.zeros((1, width), F32)], axis=0
        )
        mixed = dot(mix, features(raw))
        left = jnp.concatenate(parts(mixed[0:16] * mixed[16:32]), axis=0).T
        left_high, left_low = split(left)
        right_high, right_low = split(mixed[32:64] * mixed[64:96])
        right_high = jnp.concatenate(parts(right_high), axis=0)
        right_low = jnp.concatenate(parts(right_low), axis=0)
        every = dot(
            jnp.concatenate([right_high, right_high, right_low], axis=1),
            jnp.concatenate([left_high, left_low, left_high], axis=0),
        )
        cells = every[0:32]
        for leaf in range(1, GROUP_LEAVES):
            cells = jnp.where(lane_leaf == leaf, every[32 * leaf : 32 * leaf + 32], cells)
        cell_ref[pl.ds(pl.multiple_of(block * 128, 128), 128), :] = cells.T
        return carry

    lax.fori_loop(0, LEAF_DEV // GROUP_LEAVES, expand, 0, unroll=2)
    for c in range(3):
        total = jnp.zeros((LEAF_DEV, COEF), F32)
        for a in range(ORDER):
            piece = cell_ref[pl.ds(c * ORDER + a, LEAF_DEV, stride=16), :].astype(BF16)
            total = total + dot(piece, spread_ref[a])
        moment_ref[:, c * COEF : (c + 1) * COEF] = total.astype(BF16)

    got_ref[...] = dot(pick_ref[...], moment_ref[...]).astype(BF16)
    for direction in range(9):
        residue = 8 - direction
        rows = slice(direction * 128, (direction + 1) * 128)
        grid = dot(place_ref[rows, :], got_ref[rows, :]).astype(BF16)
        steps = (OFFSETS - residue + 8) // 9
        left = jnp.concatenate(
            [
                jnp.concatenate(
                    [grid[o * ACT_MOST : (o + 1) * ACT_MOST, c * COEF : (c + 1) * COEF] for o in range(steps)], axis=1
                )
                for c in range(3)
            ],
            axis=0,
        )
        right = jnp.concatenate([ops_ref[residue + 9 * o] for o in range(steps)], axis=0)
        outs[direction // 3][direction % 3] = dot(left, right)


def source_features(raw):
    row = iota((8, LEAF_PART), 0)
    half = jnp.where(row < 3, raw * 0.5, 0.0)
    high = half.astype(BF16).astype(F32)
    low = (half - high).astype(BF16).astype(F32)
    near = high + low
    norm = jnp.sum(near * near, axis=0, keepdims=True)
    norm_high = norm.astype(BF16).astype(F32)
    rest = norm - norm_high
    norm_mid = rest.astype(BF16).astype(F32)
    norm_low = rest - norm_mid
    first = jnp.where(
        row < 3, high, jnp.where(row == 3, norm_high, jnp.where(row == 4, norm_mid, jnp.where(row == 5, norm_low, 1.0)))
    )
    second = jnp.where(row == 3, 1.0, low)
    return jnp.concatenate([first, second, high, low], axis=0).T.astype(BF16)


def target_features(raw, shift):
    row = iota((8, LEAF_PART), 0)
    moved = jnp.where(row < 3, raw * 0.5, 0.0) + shift
    high = moved.astype(BF16).astype(F32)
    low = (moved - high).astype(BF16).astype(F32)
    near = high + low
    norm = jnp.sum(near * near, axis=0, keepdims=True) + SMOOTH
    norm_high = norm.astype(BF16).astype(F32)
    rest = norm - norm_high
    norm_mid = rest.astype(BF16).astype(F32)
    norm_low = rest - norm_mid
    high = -2.0 * high
    low = -2.0 * low
    first = jnp.where(row < 3, high, jnp.where(row < 6, 1.0, jnp.where(row == 6, norm_high, norm_mid)))
    second = jnp.where(row == 3, norm_low, high)
    return jnp.concatenate([first, second, low, low], axis=0).astype(BF16)


def source_rows(raw):
    row = iota((8, LEAF_PART), 0)
    high = raw.astype(BF16).astype(F32)
    low = pltpu.roll(raw - high, 5, 0)
    return jnp.where(row < 3, low, jnp.where(row < 6, high, 0.0)).astype(BF16)


def leaf_rows(packet_ref, slot, base=0):
    return packet_ref[pl.ds(base + slot * ROWS_LEAF, 8), :]


def effect(target, source, shift):
    kernel = lax.rsqrt(dot(source_features(source), target_features(target, shift)))
    rows = source_rows(source)
    return dot(jnp.concatenate([rows, rows], axis=1), jnp.concatenate(split(kernel), axis=0))


def self_kernel(lists_ref, index_ref, packet_ref, shift_ref, total_ref):
    total_ref[...] = jnp.zeros_like(total_ref)
    count = index_ref[ACT_MOST]
    still = jnp.zeros((8, LEAF_PART), F32)
    group = 16

    def alone(step, carry):
        results = []
        for at in range(group):
            raw = leaf_rows(packet_ref, step * group + at)
            results.append(effect(raw, raw, still))
        for at in range(group):
            total_ref[step * group + at] = results[at]
        return carry

    lax.fori_loop(0, pl.cdiv(count, group), alone, 0)
    local_pairs(lists_ref, packet_ref, shift_ref, total_ref, 0, jnp.minimum(pl.cdiv(4 * count, PAIRS), FIRST))


def local_kernel(lists_ref, index_ref, packet_ref, shift_ref, near_ref, total_ref):
    total_ref[...] = near_ref[...]
    local_pairs(lists_ref, packet_ref, shift_ref, total_ref, FIRST, pl.cdiv(4 * index_ref[ACT_MOST], PAIRS))


def local_pairs(lists_ref, packet_ref, shift_ref, total_ref, begin, end):
    def pairs(step, carry):
        results = []
        for at in range(PAIRS):
            column = step * PAIRS + at
            first = lists_ref[0, column]
            second = lists_ref[1, column]
            code = lists_ref[2, column]
            one = leaf_rows(packet_ref, first)
            other = leaf_rows(packet_ref, second)
            results.append((first, effect(one, other, shift_ref[32 + code])))
            results.append((second, effect(other, one, shift_ref[code])))
        for slot, terms in results:
            total_ref[slot] += terms
        return carry

    lax.fori_loop(begin, end, pairs, 0)


def remote_kernel(
    lists_ref,
    index_ref,
    packet_ref,
    shift_ref,
    near_ref,
    before_ref,
    after_ref,
    lower_ref,
    upper_ref,
    block_ref,
    from_lower_ref,
    from_upper_ref,
    mix_ref,
    out_ref,
    total_ref,
    local_ref,
    meta_ref,
    got_ref,
    sem,
):
    back = ((after_ref, 2), (after_ref, 1), (after_ref, 0), (upper_ref, 0))
    front = ((before_ref, 0), (before_ref, 1), (before_ref, 2), (lower_ref, 0))
    for side, (ref, place) in enumerate(back):
        meta_ref[8 * side : 8 * side + 8, :] = ref[place * PACKET + META : place * PACKET + META + 8, :].astype(jnp.int32)
    copy = pltpu.make_async_copy(meta_ref, got_ref, sem)
    copy.start()
    total_ref[...] = near_ref[...]
    out_ref[...] = jnp.zeros_like(out_ref)
    middle = slice(3 * PACKET + 3 * ACT_MOST, 3 * PACKET + 6 * ACT_MOST)
    local_ref[...] = block_ref[1] + before_ref[middle, :] + after_ref[middle, :] + from_lower_ref[...] + from_upper_ref[...]

    def all_sides(sides, target_of, source_of, code_of, sign):
        def columns(step, carry):
            picks = []
            for side, (ref, place) in enumerate(sides):
                for at in range(PCAP // 4):
                    picks.append((side, ref, place, side * PCAP + step * (PCAP // 4) + at))
            targets = [target_of(side, column) for side, ref, place, column in picks]
            live = targets[0] != DEAD
            for target in targets[1:]:
                live = live | (target != DEAD)

            @pl.when(live)
            def _():
                results = []
                for target, (side, ref, place, column) in zip(targets, picks):
                    source = leaf_rows(ref, source_of(side, column), place * PACKET)
                    shift = shift_ref[sign + code_of(side, column)]
                    results.append(effect(leaf_rows(packet_ref, target), source, shift))
                for target, terms in zip(targets, results):
                    total_ref[target] += terms

            return carry

        lax.fori_loop(0, 4, columns, 0)

    all_sides(front, lambda side, c: lists_ref[3, c], lambda side, c: lists_ref[4, c], lambda side, c: lists_ref[5, c], 32)
    copy.wait()
    all_sides(
        back,
        lambda side, c: got_ref[8 * side + 1, c],
        lambda side, c: got_ref[8 * side, c],
        lambda side, c: got_ref[8 * side + 2, c],
        0,
    )

    count = index_ref[ACT_MOST]
    row = iota((8, GROUP_LEAVES * LEAF_PART), 0)

    def finish(step, carry):
        raw = jnp.concatenate([leaf_rows(packet_ref, step * GROUP_LEAVES + at) for at in range(GROUP_LEAVES)], axis=1)
        mixed = dot(mix_ref[...], features(jnp.where(row == 6, 1.0, raw)))
        high, low = split(mixed[0:COEF] * mixed[COEF : 2 * COEF] * mixed[2 * COEF :])
        results = []
        for at in range(GROUP_LEAVES):
            rows = [local_ref[pl.ds(c * ACT_MOST + step * GROUP_LEAVES + at, 1), :] for c in range(3)]
            left_high, left_low = split(jnp.concatenate(rows + [jnp.zeros((5, COEF), F32)], axis=0))
            part = slice(at * LEAF_PART, (at + 1) * LEAF_PART)
            far = dot(
                jnp.concatenate([left_high, left_high, left_low], axis=1),
                jnp.concatenate([high[:, part], low[:, part], high[:, part]], axis=0),
            )
            near = total_ref[step * GROUP_LEAVES + at]
            results.append((near + pltpu.roll(near, 5, 0) + far)[0:3])
        for at in range(GROUP_LEAVES):
            slot = step * GROUP_LEAVES + at

            @pl.when(slot < count)
            def _(at=at, slot=slot):
                here = pl.ds(pl.multiple_of(index_ref[slot] * LEAF_PART, LEAF_PART), LEAF_PART)
                out_ref[:, here] = results[at]

        return carry

    lax.fori_loop(0, pl.cdiv(count, GROUP_LEAVES), finish, 0)


def moved(value, axis, step):
    count = lax.axis_size(axis)
    first, last = (max(0, -step), min(count, count - step))
    return lax.ppermute(value, axis, [(source, source + step) for source in range(first, last)])


VMEM = pl.BlockSpec(memory_space=pltpu.VMEM)
SMEM = pl.BlockSpec(memory_space=pltpu.SMEM)


def on_device(positions, strengths, active, m2l_list, p2p_list, local_pairs, m2l_ops):
    far_list = m2l_list.reshape(27, 128)
    near_list = p2p_list.reshape(3, 128)
    pair_list = local_pairs.reshape(3, 128)
    params = pltpu.CompilerParams(vmem_limit_bytes=VMEM_LIMIT)
    shifts = jnp.asarray(displacements())

    packet, lists, index = pl.pallas_call(
        pack_kernel,
        out_shape=(
            jax.ShapeDtypeStruct((PACKET, 128), F32),
            jax.ShapeDtypeStruct((8, 128), jnp.int32),
            jax.ShapeDtypeStruct((64,), jnp.int32),
        ),
        in_specs=[SMEM] + [VMEM] * 6,
        out_specs=(VMEM, VMEM, SMEM),
        compiler_params=params,
        name="pack",
    )(active, positions, strengths, active.reshape(1, LEAF_DEV), far_list, near_list, pair_list)

    lower = moved(packet, "dev", 1)
    upper = moved(packet, "dev", -1)

    blocks_before, blocks, blocks_after = pl.pallas_call(
        far_kernel,
        out_shape=[jax.ShapeDtypeStruct((3, 3 * ACT_MOST, COEF), F32)] * 3,
        in_specs=[VMEM] * 6,
        out_specs=[VMEM] * 3,
        scratch_shapes=[
            pltpu.VMEM((LEAF_DEV * 16, 32), F32),
            pltpu.VMEM((LEAF_DEV, 3 * COEF), BF16),
            pltpu.VMEM((9 * 128, LEAF_DEV), BF16),
            pltpu.VMEM((9 * 128, 128), BF16),
            pltpu.VMEM((9 * 128, 3 * COEF), BF16),
        ],
        compiler_params=params,
        cost_estimate=pl.CostEstimate(flops=4_000_000_000, bytes_accessed=4_000_000, transcendentals=0),
        name="moments",
    )(positions, strengths, far_list, m2l_ops, jnp.asarray(moment_rows()), jnp.asarray(spreading()))

    three = [lower, packet, upper]
    to_upper = jnp.concatenate(three + [blocks_after.reshape(-1, 128)], axis=0)
    to_lower = jnp.concatenate(three + [blocks_before.reshape(-1, 128)], axis=0)
    before = moved(to_upper, "group", 1)
    after = moved(to_lower, "group", -1)

    total_shape = jax.ShapeDtypeStruct((ACT_MOST + 1, 8, LEAF_PART), F32)
    total = pl.pallas_call(
        self_kernel,
        out_shape=total_shape,
        in_specs=[SMEM, SMEM, VMEM, VMEM],
        out_specs=VMEM,
        compiler_params=params,
        cost_estimate=pl.CostEstimate(flops=4_000_000_000, bytes_accessed=4_000_000, transcendentals=0),
        name="self_pairs",
    )(lists, index, packet, shifts)
    before, after, total = lax.optimization_barrier((before, after, total))

    rows = 3 * ACT_MOST

    def summed(step):
        base = 3 * PACKET + step * rows
        return blocks[step] + before[base : base + rows] + after[base : base + rows]

    from_lower = moved(summed(2), "dev", 1)
    from_upper = moved(summed(0), "dev", -1)

    total = pl.pallas_call(
        local_kernel,
        out_shape=total_shape,
        in_specs=[SMEM, SMEM, VMEM, VMEM, VMEM],
        out_specs=VMEM,
        compiler_params=params,
        cost_estimate=pl.CostEstimate(flops=4_000_000_000, bytes_accessed=4_000_000, transcendentals=0),
        name="local_pairs",
    )(lists, index, packet, shifts, total)
    from_lower, from_upper, total = lax.optimization_barrier((from_lower, from_upper, total))

    return pl.pallas_call(
        remote_kernel,
        out_shape=jax.ShapeDtypeStruct(positions.shape, F32),
        in_specs=[SMEM, SMEM]
        + [VMEM] * 11,
        out_specs=VMEM,
        scratch_shapes=[
            pltpu.VMEM((ACT_MOST + 1, 8, LEAF_PART), F32),
            pltpu.VMEM((rows, COEF), F32),
            pltpu.VMEM((32, 128), jnp.int32),
            pltpu.SMEM((32, 128), jnp.int32),
            pltpu.SemaphoreType.DMA,
        ],
        compiler_params=params,
        cost_estimate=pl.CostEstimate(flops=4_000_000_000, bytes_accessed=4_000_000, transcendentals=0),
        name="remote_pairs",
    )(
        lists,
        index,
        packet,
        shifts,
        total,
        before,
        after,
        lower,
        upper,
        blocks,
        from_lower,
        from_upper,
        jnp.asarray(basis_rows()),
    )


def solution(mesh):
    in_specs = (
        P(None, ("group", "dev")),
        P(None, ("group", "dev")),
        P(("group", "dev")),
        P(("group", "dev"), None, None),
        P(("group", "dev"), None, None),
        P(("group", "dev"), None, None),
        P(),
    )
    out_specs = P(None, ("group", "dev"))
    return jax.shard_map(
        on_device, mesh=mesh, in_specs=in_specs, out_specs=out_specs, check_vma=False
    )
```

time: 457 us -> 70.3 us (0.15)
  the two profiles are of different devices: /device:TPU:4 before, /device:TPU:260 now
where the time goes in v1:
time: 70.3 us; the launch traced here: 69.8 us
  Pallas kernels  38.8 us (55%)
  starting transfers between devices  20 us (28%)
  waiting for transfers between devices  5.84 us (8%)
  local copies, waits for them, and re-layouts  4.03 us (6%)
  other arithmetic  0.87 us (1%)
    ppermute x6, starting transfers between devices, moved(): lax.ppermute(value, axis, [(source, source + step) for source in range(fi...  20 us
    pallas_call x1, Pallas kernels, on_device(): pl.pallas_call(far_kernel, out_shape=[jax.ShapeDtypeStruct((3, 3 * ACT_MO...  17.2 us
    pallas_call x1, Pallas kernels, on_device(): pl.pallas_call(remote_kernel, out_shape=jax.ShapeDtypeStruct(positions.sh...  10.9 us
    ppermute x6, waiting for transfers between devices, moved(): lax.ppermute(value, axis, [(source, source + step) for source in range(fi...  5.84 us
    pallas_call x1, Pallas kernels, on_device(): pl.pallas_call(self_kernel, out_shape=total_shape, in_specs=[SMEM, SMEM,...  5.52 us
    unnamed x25, local copies, waits for them, and re-layouts  4.02 us
    pallas_call x1, Pallas kernels, on_device(): pl.pallas_call(local_kernel, out_shape=total_shape, in_specs=[SMEM, SMEM,...  3.34 us
    pallas_call x1, Pallas kernels, on_device(): pl.pallas_call(pack_kernel, out_shape=(jax.ShapeDtypeStruct((PACKET, 128)...  1.78 us
  transfers between devices with their start and end apart: 6, of which 2 were waited for; matrix products, arithmetic and copies ran while one was open for 0% of the time, Pallas kernels for 37%

profile of v1, /device:TPU:260, one launch (start us, length us, event | category | flops | bytes accessed | tf_op | source)
XLA Modules:
  0.0 69.8 jit_solution(2083382808278136384)
XLA Ops:
  0.0 0.8 %reduce = s32[3,1152]{1,0:T(4,128)S(1)} reduce(s32[1,3,1152]{2,0,1:T(1,128)} %param.14, s32[]{:T(128)} %constant.16), dimensions={0}, to_apply=%param.14.reduce_sub_computation | reduce | bytes 27652 | tf_op args[3]
  0.8 0.0 copy-start.8
  0.9 0.0 copy-start.4
  0.9 0.7 copy-done.4
  1.5 1.0 %copy-done = f32[3,32768]{1,0:T(4,128)S(1)} copy-done((f32[3,32768]{1,0:T(4,128)S(1)}, f32[3,32768]{1,0:T(4,128)}, u32[]{:S(2)}) %copy-start) | copy-done | bytes 393240
  2.6 1.0 %copy-done.2 = f32[3,32768]{1,0:T(4,128)S(1)} copy-done((f32[3,32768]{1,0:T(4,128)S(1)}, f32[3,32768]{1,0:T(4,128)}, u32[]{:S(2)}) %copy-start.2) | copy-done | bytes 393240
  3.6 1.8 %pack.1 = (f32[200,128]{1,0:T(8,128)S(1)}, s32[8,128]{1,0:T(8,128)S(1)}, s32[64]{0:T(128)S(1)}) custom-call(s32[256]{0:T(256)S(1)} %copy-done.4, f32[3,32768]{1,0:T(4,128)S(1)} %copy-done, f32[3,32768]{1,0:T(4,128)S(1)} %copy-done.2, s32[1,256]{1,0:T(1,128)S(1)} %bitcast.17, s32[27,128]{1,0:T(8,128)S(1)} %reshape.19.far_ref, ...), custom_call_target="tpu_custom_call" | custom-call | tf_op jit(solution)/shard_map/pack/pallas_call | solution.py:461
  5.4 4.5 %collective-permute-start.1 = (f32[200,128]{1,0:T(8,128)S(1)}, f32[200,128]{1,0:T(8,128)S(1)}, u32[]{:S(2)}, u32[]{:S(2)}) collective-permute-start(f32[200,128]{1,0:T(8,128)S(1)} %get-tuple-element.19.packet_ref), channel_id=1, source_target_pairs={{1,0},{2,1},{3,2},{4,3},{5,4},{6,5},{7,6},{8,7},{9,8},{10,9},{11,1... | collective-permute-start | bytes 307208 | tf_op jit(solution)/shard_map/ppermute | solution.py:447
  9.9 1.9 %collective-permute-start = (f32[200,128]{1,0:T(8,128)S(1)}, f32[200,128]{1,0:T(8,128)S(1)}, u32[]{:S(2)}, u32[]{:S(2)}) collective-permute-start(f32[200,128]{1,0:T(8,128)S(1)} %get-tuple-element.19.packet_ref), channel_id=1, source_target_pairs={{0,1},{1,2},{2,3},{3,4},{4,5},{5,6},{6,7},{7,8},{8,9},{9,10},{10,1... | collective-permute-start | bytes 307208 | tf_op jit(solution)/shard_map/ppermute | solution.py:447
  11.9 0.0 copy-start.5
  11.9 1.2 %copy-done.5 = bf16[32,128,128]{2,1,0:T(8,128)(2,1)S(1)} copy-done((bf16[32,128,128]{2,1,0:T(8,128)(2,1)S(1)}, bf16[32,128,128]{2,1,0:T(8,128)(2,1)}, u32[]{:S(2)}) %copy-start.5) | copy-done | bytes 1048600
  13.1 17.2 %moments.1 = (f32[3,96,128]{2,1,0:T(8,128)S(1)}, f32[3,96,128]{2,1,0:T(8,128)S(1)}, f32[3,96,128]{2,1,0:T(8,128)S(1)}) custom-call(f32[3,32768]{1,0:T(4,128)S(1)} %copy-done.1, f32[3,32768]{1,0:T(4,128)S(1)} %copy-done.3, s32[27,128]{1,0:T(8,128)S(1)} %reshape.19.far_ref, bf16[32,128,128]{2,1,0:T(8,128)(2,1)S(1)} %copy-done.5, bf16[96,96]{1,0:T(8,128)(2,1)S(1)} %copy-done.9, ...), custom_call_target="tpu_custom_call" | custom-call | flops 4000000000 | bytes 4000000 | tf_op jit(solution)/shard_map/moments/pallas_call | solution.py:477
  30.4 0.0 copy-start.6
  30.4 0.1 pad_maximum_fusion.2
  30.4 1.9 %collective-permute-start.3 = (f32[888,128]{1,0:T(8,128)S(1)}, f32[888,128]{1,0:T(8,128)S(1)}, u32[]{:S(2)}, u32[]{:S(2)}) collective-permute-start(f32[888,128]{1,0:T(8,128)S(1)} %get-tuple-element.31), channel_id=1, source_target_pairs={{64,0},{128,64},{192,128},{256,192},{320,256},{384,320},{448,384},... | collective-permute-start | bytes 1363976 | tf_op jit(solution)/shard_map/ppermute | solution.py:447
  32.4 2.4 %collective-permute-start.2 = (f32[888,128]{1,0:T(8,128)S(1)}, f32[888,128]{1,0:T(8,128)S(1)}, u32[]{:S(2)}, u32[]{:S(2)}) collective-permute-start(f32[888,128]{1,0:T(8,128)S(1)} %get-tuple-element.32), channel_id=1, source_target_pairs={{0,64},{64,128},{128,192},{192,256},{256,320},{320,384},{384,448},... | collective-permute-start | bytes 1363976 | tf_op jit(solution)/shard_map/ppermute | solution.py:447
  34.8 5.5 %self_pairs.1.near_ref = f32[33,8,128]{2,1,0:T(8,128)S(1)} custom-call(s32[8,128]{1,0:T(8,128)S(1)} %get-tuple-element.17.lists_ref, s32[64]{0:T(128)S(1)} %get-tuple-element.18.index_ref, f32[200,128]{1,0:T(8,128)S(1)} %get-tuple-element.19.packet_ref, f32[64,8,128]{2,1,0:T(8,128)S(1)} %copy-done.6), custom_call_target="tpu_custom_call" | custom-call | flops 4000000000 | bytes 4000000 | tf_op jit(solution)/shard_map/self_pairs/pallas_call | solution.py:501
  40.3 1.8 %collective-permute-done.2.before_ref = f32[888,128]{1,0:T(8,128)S(1)} collective-permute-done((f32[888,128]{1,0:T(8,128)S(1)}, f32[888,128]{1,0:T(8,128)S(1)}, u32[]{:S(2)}, u32[]{:S(2)}) %collective-permute-start.2) | collective-permute-done | bytes 454688 | tf_op jit(solution)/shard_map/ppermute | solution.py:447
  42.2 7.2 %collective-permute-start.5 = (f32[96,128]{1,0:T(8,128)S(1)}, f32[96,128]{1,0:T(8,128)S(1)}, u32[]{:S(2)}, u32[]{:S(2)}) collective-permute-start(f32[96,128]{1,0:T(8,128)S(1)} %get-tuple-element.29), channel_id=1, source_target_pairs={{1,0},{2,1},{3,2},{4,3},{5,4},{6,5},{7,6},{8,7},{9,8},{10,9},{11,1... | collective-permute-start | bytes 147464 | tf_op jit(solution)/shard_map/ppermute | solution.py:447
  49.4 0.0 copy-start.7
  49.4 2.1 %collective-permute-start.4 = (f32[96,128]{1,0:T(8,128)S(1)}, f32[96,128]{1,0:T(8,128)S(1)}, u32[]{:S(2)}, u32[]{:S(2)}) collective-permute-start(f32[96,128]{1,0:T(8,128)S(1)} %get-tuple-element.30), channel_id=1, source_target_pairs={{0,1},{1,2},{2,3},{3,4},{4,5},{5,6},{6,7},{7,8},{8,9},{9,10},{10,1... | collective-permute-start | bytes 147464 | tf_op jit(solution)/shard_map/ppermute | solution.py:447
  51.5 3.3 %local_pairs.1.near_ref = f32[33,8,128]{2,1,0:T(8,128)S(1)} custom-call(s32[8,128]{1,0:T(8,128)S(1)} %get-tuple-element.17.lists_ref, s32[64]{0:T(128)S(1)} %get-tuple-element.18.index_ref, f32[200,128]{1,0:T(8,128)S(1)} %get-tuple-element.19.packet_ref, f32[64,8,128]{2,1,0:T(8,128)S(1)} %copy-done.6, f32[33,8,128]{2,1,0:T(8,128)S(1)} %self_pairs.1.near_ref), custom_call_target="tpu_custom_call" | custom-call | flops 4000000000 | bytes 4000000 | tf_op jit(solution)/shard_map/local_pairs/pallas_call | solution.py:521
  54.8 4.0 %collective-permute-done.4.from_lower_ref = f32[96,128]{1,0:T(8,128)S(1)} collective-permute-done((f32[96,128]{1,0:T(8,128)S(1)}, f32[96,128]{1,0:T(8,128)S(1)}, u32[]{:S(2)}, u32[]{:S(2)}) %collective-permute-start.4) | collective-permute-done | bytes 49184 | tf_op jit(solution)/shard_map/ppermute | solution.py:447
  58.9 10.9 %remote_pairs.1 = f32[3,32768]{1,0:T(4,128)} custom-call(s32[8,128]{1,0:T(8,128)S(1)} %get-tuple-element.17.lists_ref, s32[64]{0:T(128)S(1)} %get-tuple-element.18.index_ref, f32[200,128]{1,0:T(8,128)S(1)} %get-tuple-element.19.packet_ref, f32[64,8,128]{2,1,0:T(8,128)S(1)} %copy-done.6, f32[33,8,128]{2,1,0:T(8,128)S(1)} %local_pairs.1.near_ref, ...), custom_call_target="tpu_custom_call" | custom-call | flops 4000000000 | bytes 4000000 | tf_op jit(solution)/shard_map/remote_pairs/pallas_call | solution.py:532
  (22 shorter events, 0.1 us)
Async XLA Ops:
  0.0 0.8 %copy-start.10 = (s32[1,3,128]{2,0,1:T(1,128)S(1)}, s32[1,3,128]{2,0,1:T(1,128)}, u32[]{:S(2)}) copy-start(s32[1,3,128]{2,0,1:T(1,128)} %param.16) | copy-start | bytes 4612
  0.0 0.8 %copy-start.11 = (s32[1,3,128]{2,0,1:T(1,128)S(1)}, s32[1,3,128]{2,0,1:T(1,128)}, u32[]{:S(2)}) copy-start(s32[1,3,128]{2,0,1:T(1,128)} %param.15) | copy-start | bytes 4612
  0.0 11.8 %copy-start.9 = (bf16[96,96]{1,0:T(8,128)(2,1)S(1)}, bf16[96,96]{1,0:T(8,128)(2,1)}, u32[]{:S(2)}) copy-start(bf16[96,96]{1,0:T(8,128)(2,1)} %constant.9.clone.mix_ref) | copy-start | bytes 55300
  0.8 11.0 %copy-start.8 = (bf16[5,32,128]{2,1,0:T(8,128)(2,1)S(1)}, bf16[5,32,128]{2,1,0:T(8,128)(2,1)}, u32[]{:S(2)}) copy-start(bf16[5,32,128]{2,1,0:T(8,128)(2,1)} %constant.10.clone.spread_ref) | copy-start | bytes 122884
  0.9 0.7 copy-start.4
  1.5 1.0 %copy-start = (f32[3,32768]{1,0:T(4,128)S(1)}, f32[3,32768]{1,0:T(4,128)}, u32[]{:S(2)}) copy-start(f32[3,32768]{1,0:T(4,128)} %pos_ref.3) | copy-start | bytes 1179652
  2.6 1.0 %copy-start.2 = (f32[3,32768]{1,0:T(4,128)S(1)}, f32[3,32768]{1,0:T(4,128)}, u32[]{:S(2)}) copy-start(f32[3,32768]{1,0:T(4,128)} %str_ref.3) | copy-start | bytes 1179652
  3.6 8.2 %copy-start.1 = (f32[3,32768]{1,0:T(4,128)S(1)}, f32[3,32768]{1,0:T(4,128)}, u32[]{:S(2)}) copy-start(f32[3,32768]{1,0:T(4,128)} %pos_ref.3) | copy-start | bytes 1179652
  3.6 8.2 %copy-start.3 = (f32[3,32768]{1,0:T(4,128)S(1)}, f32[3,32768]{1,0:T(4,128)}, u32[]{:S(2)}) copy-start(f32[3,32768]{1,0:T(4,128)} %str_ref.3) | copy-start | bytes 1179652
  5.4 24.9 %collective-permute-start.1 = (f32[200,128]{1,0:T(8,128)S(1)}, f32[200,128]{1,0:T(8,128)S(1)}, u32[]{:S(2)}, u32[]{:S(2)}) collective-permute-start(f32[200,128]{1,0:T(8,128)S(1)} %get-tuple-element.19.packet_ref), channel_id=1, source_target_pairs={{1,0},{2,1},{3,2},{4,3},{5,4},{6,5},{7,6},{8,7},{9,8},{10,9},{11,1... | collective-permute-start | bytes 307208 | tf_op jit(solution)/shard_map/ppermute | solution.py:447
  9.9 20.5 %collective-permute-start = (f32[200,128]{1,0:T(8,128)S(1)}, f32[200,128]{1,0:T(8,128)S(1)}, u32[]{:S(2)}, u32[]{:S(2)}) collective-permute-start(f32[200,128]{1,0:T(8,128)S(1)} %get-tuple-element.19.packet_ref), channel_id=1, source_target_pairs={{0,1},{1,2},{2,3},{3,4},{4,5},{5,6},{6,7},{7,8},{8,9},{9,10},{10,1... | collective-permute-start | bytes 307208 | tf_op jit(solution)/shard_map/ppermute | solution.py:447
  11.9 1.2 %copy-start.5 = (bf16[32,128,128]{2,1,0:T(8,128)(2,1)S(1)}, bf16[32,128,128]{2,1,0:T(8,128)(2,1)}, u32[]{:S(2)}) copy-start(bf16[32,128,128]{2,1,0:T(8,128)(2,1)} %ops_ref.1) | copy-start | bytes 3145732
  30.4 4.4 %copy-start.6 = (f32[64,8,128]{2,1,0:T(8,128)S(1)}, f32[64,8,128]{2,1,0:T(8,128)}, u32[]{:S(2)}) copy-start(f32[64,8,128]{2,1,0:T(8,128)} %constant.8.clone.shift_ref) | copy-start | bytes 786436
  30.4 9.9 %collective-permute-start.3 = (f32[888,128]{1,0:T(8,128)S(1)}, f32[888,128]{1,0:T(8,128)S(1)}, u32[]{:S(2)}, u32[]{:S(2)}) collective-permute-start(f32[888,128]{1,0:T(8,128)S(1)} %get-tuple-element.31), channel_id=1, source_target_pairs={{64,0},{128,64},{192,128},{256,192},{320,256},{384,320},{448,384},... | collective-permute-start | bytes 1363976 | tf_op jit(solution)/shard_map/ppermute | solution.py:447
  32.4 9.8 %collective-permute-start.2 = (f32[888,128]{1,0:T(8,128)S(1)}, f32[888,128]{1,0:T(8,128)S(1)}, u32[]{:S(2)}, u32[]{:S(2)}) collective-permute-start(f32[888,128]{1,0:T(8,128)S(1)} %get-tuple-element.32), channel_id=1, source_target_pairs={{0,64},{64,128},{128,192},{192,256},{256,320},{320,384},{384,448},... | collective-permute-start | bytes 1363976 | tf_op jit(solution)/shard_map/ppermute | solution.py:447
  42.2 12.7 %collective-permute-start.5 = (f32[96,128]{1,0:T(8,128)S(1)}, f32[96,128]{1,0:T(8,128)S(1)}, u32[]{:S(2)}, u32[]{:S(2)}) collective-permute-start(f32[96,128]{1,0:T(8,128)S(1)} %get-tuple-element.29), channel_id=1, source_target_pairs={{1,0},{2,1},{3,2},{4,3},{5,4},{6,5},{7,6},{8,7},{9,8},{10,9},{11,1... | collective-permute-start | bytes 147464 | tf_op jit(solution)/shard_map/ppermute | solution.py:447
  49.4 9.5 %copy-start.7 = (bf16[384,96]{1,0:T(8,128)(2,1)S(1)}, bf16[384,96]{1,0:T(8,128)(2,1)}, u32[]{:S(2)}) copy-start(bf16[384,96]{1,0:T(8,128)(2,1)} %constant.11.clone.mix_ref) | copy-start | bytes 221188
  49.4 9.4 %collective-permute-start.4 = (f32[96,128]{1,0:T(8,128)S(1)}, f32[96,128]{1,0:T(8,128)S(1)}, u32[]{:S(2)}, u32[]{:S(2)}) collective-permute-start(f32[96,128]{1,0:T(8,128)S(1)} %get-tuple-element.30), channel_id=1, source_target_pairs={{0,1},{1,2},{2,3},{3,4},{4,5},{5,6},{6,7},{7,8},{8,9},{9,10},{10,1... | collective-permute-start | bytes 147464 | tf_op jit(solution)/shard_map/ppermute | solution.py:447

commit v2 on v1

--- a/solution.py
+++ b/solution.py
@@ -20,13 +20,14 @@
 ROWS_LEAF = 6
 META = ROWS_LEAF * ACT_MOST
 PACKET = META + 8
+ROWS_FAR = 3 * ACT_MOST
 GROUP_LEAVES = 8
 PAIRS = 16
 FIRST = 4
 SMOOTH = 0.04
 FORWARD_GROUP = (-1, -1, -1, 0)
 FORWARD_MEMBER = (-1, 0, 1, -1)
-VMEM_LIMIT = 40 * 1024 * 1024
+VMEM_LIMIT = 56 * 1024 * 1024
 
 F32 = jnp.float32
 BF16 = jnp.bfloat16
@@ -90,15 +91,16 @@
     return table.astype(ml_dtypes.bfloat16)
 
 
-def displacements():
-    table = np.zeros((2, 32, 8, LEAF_PART), np.float32)
+def displacements(shift_ref):
+    row = iota((8, LEAF_PART), 0)
     for code in range(26):
         shifted = code + (1 if code >= 13 else 0)
         vector = (shifted // 9 - 1, shifted // 3 % 3 - 1, shifted % 3 - 1)
+        value = jnp.zeros((8, LEAF_PART), F32)
         for dim in range(3):
-            table[0, code, dim] = vector[dim]
-            table[1, code, dim] = -vector[dim]
-    return table.reshape(64, 8, LEAF_PART)
+            value = jnp.where(row == dim, float(vector[dim]), value)
+        shift_ref[code] = value
+        shift_ref[32 + code] = -value
 
 
 def features(raw):
@@ -110,8 +112,7 @@
 
 
 def presence(targets, classes, residue):
-    leaves = iota((LEAF_DEV, 128), 0)
-    hit = (leaves == targets).astype(F32).astype(BF16)
+    hit = (iota((LEAF_DEV, 128), 0) == targets).astype(F32).astype(BF16)
     counted = jnp.broadcast_to((classes == residue) & (targets >= 0), (16, 128))
     return dot(counted.astype(F32).astype(BF16), hit, NT).astype(BF16)
 
@@ -120,23 +121,59 @@
     return (iota((LEAF_DEV, 128), 0) < targets).astype(F32).astype(BF16)
 
 
-def pack_kernel(
-    flags_ref, pos_ref, str_ref, active_ref, far_ref, near_ref, local_ref, packet_ref, lists_ref, index_ref
+def front_kernel(
+    flags_ref,
+    active_ref,
+    far_flat,
+    near_flat,
+    pairs_flat,
+    mix_ref,
+    spread_ref,
+    pos_hbm,
+    str_hbm,
+    ops_hbm,
+    to_upper_ref,
+    to_lower_ref,
+    stay_ref,
+    lists_ref,
+    index_ref,
+    pos_ref,
+    str_ref,
+    ops_ref,
+    cell_ref,
+    moment_ref,
+    pick_ref,
+    place_ref,
+    got_ref,
+    left_ref,
+    high_ref,
+    low_ref,
+    far_ref,
+    near_ref,
+    pairs_ref,
+    sems,
 ):
+    copies = [
+        pltpu.make_async_copy(pos_hbm, pos_ref, sems.at[0]),
+        pltpu.make_async_copy(str_hbm, str_ref, sems.at[1]),
+        pltpu.make_async_copy(ops_hbm, ops_ref, sems.at[2]),
+    ]
+    for copy in copies:
+        copy.start()
+    for flat, ref, blocks in ((far_flat, far_ref, 9), (near_flat, near_ref, 1), (pairs_flat, pairs_ref, 1)):
+        for kind in range(3):
+            for block in range(blocks):
+                row = kind * blocks + block
+                ref[row : row + 1, :] = flat[kind, :, block * 128 : (block + 1) * 128]
+
     def enter(leaf, count):
         index_ref[count] = leaf
         return count + flags_ref[leaf]
 
     for slot in range(ACT_MOST):
         index_ref[slot] = 0
-    count = lax.fori_loop(0, LEAF_DEV, enter, 0, unroll=8)
+    count = lax.fori_loop(0, LEAF_DEV, enter, 0, unroll=16)
     index_ref[ACT_MOST] = count
-    for slot in range(ACT_MOST):
-        leaf = index_ref[slot]
-        leaf = jnp.where(slot < count, leaf, 0)
-        here = pl.ds(pl.multiple_of(leaf * LEAF_PART, LEAF_PART), LEAF_PART)
-        packet_ref[ROWS_LEAF * slot : ROWS_LEAF * slot + 3, :] = pos_ref[:, here]
-        packet_ref[ROWS_LEAF * slot + 3 : ROWS_LEAF * slot + 6, :] = str_ref[:, here]
 
     own = jnp.broadcast_to(active_ref[...].astype(F32), (16, LEAF_DEV)).astype(BF16)
 
@@ -150,29 +187,22 @@
     second_slot = jnp.full((1, 128), DEAD, jnp.int32)
     for side in range(4):
         direction = 3 * (FORWARD_GROUP[side] + 1) + FORWARD_MEMBER[side] + 1
-        there = presence(far_ref[18 + direction : 19 + direction, :], far_ref[9 + direction : 10 + direction, :], 8 - direction)
+        there = presence(
+            far_ref[18 + direction : 19 + direction, :], far_ref[9 + direction : 10 + direction, :], 8 - direction
+        )
         rank = dot(there, under)[0:1].astype(jnp.int32)
         mine = (lanes >= side * PCAP) & (lanes < (side + 1) * PCAP) & (second >= 0)
         second_slot = jnp.where(mine, rank, second_slot)
     first_slot = own_slot(near_ref[0:1, :])
     codes = near_ref[2:3, :]
-    lists_ref[0:1, :] = own_slot(local_ref[0:1, :])
-    lists_ref[1:2, :] = own_slot(local_ref[1:2, :])
-    lists_ref[2:3, :] = local_ref[2:3, :]
+    lists_ref[0:1, :] = own_slot(pairs_ref[0:1, :])
+    lists_ref[1:2, :] = own_slot(pairs_ref[1:2, :])
+    lists_ref[2:3, :] = pairs_ref[2:3, :]
     lists_ref[3:4, :] = first_slot
     lists_ref[4:5, :] = second_slot
     lists_ref[5:6, :] = codes
     lists_ref[6:8, :] = jnp.zeros((2, 128), jnp.int32)
-    packet_ref[META : META + 1, :] = first_slot.astype(F32)
-    packet_ref[META + 1 : META + 2, :] = second_slot.astype(F32)
-    packet_ref[META + 2 : META + 3, :] = codes.astype(F32)
-    packet_ref[META + 3 :, :] = jnp.zeros((5, 128), F32)
-
-
-def far_kernel(
-    pos_ref, str_ref, far_ref, ops_ref, mix_ref, spread_ref, *rest
-):
-    outs, (cell_ref, moment_ref, pick_ref, place_ref, got_ref) = rest[:3], rest[3:]
+
     empty = jnp.zeros((7, 128), jnp.int32)
     classes = far_ref[9:18, :]
     targets = far_ref[18:27, :]
@@ -192,6 +222,20 @@
         place_ref[rows, :] = (iota((128, 128), 0) == key).astype(F32).astype(BF16)
         pick_ref[rows, :] = (sources[:, direction : direction + 1] == leaves).astype(F32).astype(BF16)
 
+    copies[0].wait()
+    copies[1].wait()
+    for ref in (to_upper_ref, to_lower_ref):
+        ref[META : META + 1, :] = first_slot.astype(F32)
+        ref[META + 1 : META + 2, :] = second_slot.astype(F32)
+        ref[META + 2 : META + 3, :] = codes.astype(F32)
+        ref[META + 3 : PACKET, :] = jnp.zeros((5, 128), F32)
+    for slot in range(ACT_MOST):
+        leaf = jnp.where(slot < count, index_ref[slot], 0)
+        here = pl.ds(pl.multiple_of(leaf * LEAF_PART, LEAF_PART), LEAF_PART)
+        for ref in (to_upper_ref, to_lower_ref):
+            ref[ROWS_LEAF * slot : ROWS_LEAF * slot + 3, :] = pos_ref[:, here]
+            ref[ROWS_LEAF * slot + 3 : ROWS_LEAF * slot + 6, :] = str_ref[:, here]
+
     mix = mix_ref[...]
     width = GROUP_LEAVES * LEAF_PART
     lane_leaf = iota((32, 128), 1) // 16
@@ -205,11 +249,19 @@
             [pos_ref[:, here], str_ref[:, here], jnp.ones((1, width), F32), jnp.zeros((1, width), F32)], axis=0
         )
         mixed = dot(mix, features(raw))
-        left = jnp.concatenate(parts(mixed[0:16] * mixed[16:32]), axis=0).T
+        left_ref[pl.ds(pl.multiple_of(block * 128, 128), 128), :] = jnp.concatenate(parts(mixed[0:16] * mixed[16:32]), axis=0)
+        right_high, right_low = split(mixed[32:64] * mixed[64:96])
+        rows = pl.ds(pl.multiple_of(block * 256, 256), 256)
+        high_ref[rows, :] = jnp.concatenate(parts(right_high), axis=0)
+        low_ref[rows, :] = jnp.concatenate(parts(right_low), axis=0)
+        return carry
+
+    def contract(block, carry):
+        left = left_ref[pl.ds(pl.multiple_of(block * 128, 128), 128), :].T
         left_high, left_low = split(left)
-        right_high, right_low = split(mixed[32:64] * mixed[64:96])
-        right_high = jnp.concatenate(parts(right_high), axis=0)
-        right_low = jnp.concatenate(parts(right_low), axis=0)
+        rows = pl.ds(pl.multiple_of(block * 256, 256), 256)
+        right_high = high_ref[rows, :]
+        right_low = low_ref[rows, :]
         every = dot(
             jnp.concatenate([right_high, right_high, right_low], axis=1),
             jnp.concatenate([left_high, left_low, left_high], axis=0),
@@ -220,7 +272,8 @@
         cell_ref[pl.ds(pl.multiple_of(block * 128, 128), 128), :] = cells.T
         return carry
 
-    lax.fori_loop(0, LEAF_DEV // GROUP_LEAVES, expand, 0, unroll=2)
+    lax.fori_loop(0, LEAF_DEV // GROUP_LEAVES, expand, 0, unroll=8)
+    lax.fori_loop(0, LEAF_DEV // GROUP_LEAVES, contract, 0, unroll=8)
     for c in range(3):
         total = jnp.zeros((LEAF_DEV, COEF), F32)
         for a in range(ORDER):
@@ -228,6 +281,7 @@
             total = total + dot(piece, spread_ref[a])
         moment_ref[:, c * COEF : (c + 1) * COEF] = total.astype(BF16)
 
+    copies[2].wait()
     got_ref[...] = dot(pick_ref[...], moment_ref[...]).astype(BF16)
     for direction in range(9):
         residue = 8 - direction
@@ -244,7 +298,12 @@
             axis=0,
         )
         right = jnp.concatenate([ops_ref[residue + 9 * o] for o in range(steps)], axis=0)
-        outs[direction // 3][direction % 3] = dot(left, right)
+        along, across = direction // 3, direction % 3
+        if across == 1:
+            stay_ref[along] = dot(left, right)
+        else:
+            ref = to_lower_ref if across == 0 else to_upper_ref
+            ref[PACKET + along * ROWS_FAR : PACKET + (along + 1) * ROWS_FAR, :] = dot(left, right)
 
 
 def source_features(raw):
@@ -300,7 +359,8 @@
     return dot(jnp.concatenate([rows, rows], axis=1), jnp.concatenate(split(kernel), axis=0))
 
 
-def self_kernel(lists_ref, index_ref, packet_ref, shift_ref, total_ref):
+def self_kernel(lists_ref, index_ref, packet_ref, total_ref, shift_ref):
+    displacements(shift_ref)
     total_ref[...] = jnp.zeros_like(total_ref)
     count = index_ref[ACT_MOST]
     still = jnp.zeros((8, LEAF_PART), F32)
@@ -319,7 +379,8 @@
     local_pairs(lists_ref, packet_ref, shift_ref, total_ref, 0, jnp.minimum(pl.cdiv(4 * count, PAIRS), FIRST))
 
 
-def local_kernel(lists_ref, index_ref, packet_ref, shift_ref, near_ref, total_ref):
+def local_kernel(lists_ref, index_ref, packet_ref, near_ref, total_ref, shift_ref):
+    displacements(shift_ref)
     total_ref[...] = near_ref[...]
     local_pairs(lists_ref, packet_ref, shift_ref, total_ref, FIRST, pl.cdiv(4 * index_ref[ACT_MOST], PAIRS))
 
@@ -343,23 +404,29 @@
     lax.fori_loop(begin, end, pairs, 0)
 
 
+def relay_kernel(lower_ref, own_ref, upper_ref, stay_ref, to_after_ref, to_before_ref):
+    for ref, along in ((to_after_ref, 2), (to_before_ref, 0)):
+        for place, source in enumerate((lower_ref, own_ref, upper_ref)):
+            ref[place * PACKET : (place + 1) * PACKET, :] = source[0:PACKET, :]
+        rows = slice(PACKET + along * ROWS_FAR, PACKET + (along + 1) * ROWS_FAR)
+        ref[3 * PACKET :, :] = stay_ref[along] + lower_ref[rows, :] + upper_ref[rows, :]
+
+
 def remote_kernel(
     lists_ref,
     index_ref,
     packet_ref,
-    shift_ref,
     near_ref,
     before_ref,
     after_ref,
     lower_ref,
     upper_ref,
-    block_ref,
-    from_lower_ref,
-    from_upper_ref,
+    stay_ref,
     mix_ref,
     out_ref,
     total_ref,
     local_ref,
+    shift_ref,
     meta_ref,
     got_ref,
     sem,
@@ -370,10 +437,13 @@
         meta_ref[8 * side : 8 * side + 8, :] = ref[place * PACKET + META : place * PACKET + META + 8, :].astype(jnp.int32)
     copy = pltpu.make_async_copy(meta_ref, got_ref, sem)
     copy.start()
+    displacements(shift_ref)
     total_ref[...] = near_ref[...]
     out_ref[...] = jnp.zeros_like(out_ref)
-    middle = slice(3 * PACKET + 3 * ACT_MOST, 3 * PACKET + 6 * ACT_MOST)
-    local_ref[...] = block_ref[1] + before_ref[middle, :] + after_ref[middle, :] + from_lower_ref[...] + from_upper_ref[...]
+    rows = slice(PACKET + ROWS_FAR, PACKET + 2 * ROWS_FAR)
+    local_ref[...] = (
+        stay_ref[1] + lower_ref[rows, :] + upper_ref[rows, :] + before_ref[3 * PACKET :, :] + after_ref[3 * PACKET :, :]
+    )
 
     def all_sides(sides, target_of, source_of, code_of, sign):
         def columns(step, carry):
@@ -449,117 +519,119 @@
 
 VMEM = pl.BlockSpec(memory_space=pltpu.VMEM)
 SMEM = pl.BlockSpec(memory_space=pltpu.SMEM)
+HBM = pl.BlockSpec(memory_space=pltpu.HBM)
 
 
 def on_device(positions, strengths, active, m2l_list, p2p_list, local_pairs, m2l_ops):
-    far_list = m2l_list.reshape(27, 128)
-    near_list = p2p_list.reshape(3, 128)
-    pair_list = local_pairs.reshape(3, 128)
+    far_list = jnp.transpose(m2l_list, (1, 0, 2))
+    near_list = jnp.transpose(p2p_list, (1, 0, 2))
+    pair_list = jnp.transpose(local_pairs, (1, 0, 2))
     params = pltpu.CompilerParams(vmem_limit_bytes=VMEM_LIMIT)
-    shifts = jnp.asarray(displacements())
-
-    packet, lists, index = pl.pallas_call(
-        pack_kernel,
+    small = pltpu.CompilerParams(vmem_limit_bytes=16 * 1024 * 1024)
+    shifts = pltpu.VMEM((64, 8, LEAF_PART), F32)
+
+    leaf_columns = positions.shape[1]
+    message = jax.ShapeDtypeStruct((PACKET + 3 * ROWS_FAR, 128), F32)
+    to_upper, to_lower, stay, lists, index = pl.pallas_call(
+        front_kernel,
         out_shape=(
-            jax.ShapeDtypeStruct((PACKET, 128), F32),
+            message,
+            message,
+            jax.ShapeDtypeStruct((3, ROWS_FAR, COEF), F32),
             jax.ShapeDtypeStruct((8, 128), jnp.int32),
             jax.ShapeDtypeStruct((64,), jnp.int32),
         ),
-        in_specs=[SMEM] + [VMEM] * 6,
-        out_specs=(VMEM, VMEM, SMEM),
-        compiler_params=params,
-        name="pack",
-    )(active, positions, strengths, active.reshape(1, LEAF_DEV), far_list, near_list, pair_list)
-
-    lower = moved(packet, "dev", 1)
-    upper = moved(packet, "dev", -1)
-
-    blocks_before, blocks, blocks_after = pl.pallas_call(
-        far_kernel,
-        out_shape=[jax.ShapeDtypeStruct((3, 3 * ACT_MOST, COEF), F32)] * 3,
-        in_specs=[VMEM] * 6,
-        out_specs=[VMEM] * 3,
+        in_specs=[SMEM] + [VMEM] * 6 + [HBM] * 3,
+        out_specs=(VMEM, VMEM, VMEM, VMEM, SMEM),
         scratch_shapes=[
+            pltpu.VMEM((3, leaf_columns), F32),
+            pltpu.VMEM((3, leaf_columns), F32),
+            pltpu.VMEM((OFFSETS, COEF, COEF), BF16),
             pltpu.VMEM((LEAF_DEV * 16, 32), F32),
             pltpu.VMEM((LEAF_DEV, 3 * COEF), BF16),
             pltpu.VMEM((9 * 128, LEAF_DEV), BF16),
             pltpu.VMEM((9 * 128, 128), BF16),
             pltpu.VMEM((9 * 128, 3 * COEF), BF16),
+            pltpu.VMEM((LEAF_DEV * 16, LEAF_PART), F32),
+            pltpu.VMEM((LEAF_DEV * 32, LEAF_PART), BF16),
+            pltpu.VMEM((LEAF_DEV * 32, LEAF_PART), BF16),
+            pltpu.VMEM((32, 128), jnp.int32),
+            pltpu.VMEM((8, 128), jnp.int32),
+            pltpu.VMEM((8, 128), jnp.int32),
+            pltpu.SemaphoreType.DMA((3,)),
         ],
         compiler_params=params,
-        cost_estimate=pl.CostEstimate(flops=4_000_000_000, bytes_accessed=4_000_000, transcendentals=0),
-        name="moments",
-    )(positions, strengths, far_list, m2l_ops, jnp.asarray(moment_rows()), jnp.asarray(spreading()))
-
-    three = [lower, packet, upper]
-    to_upper = jnp.concatenate(three + [blocks_after.reshape(-1, 128)], axis=0)
-    to_lower = jnp.concatenate(three + [blocks_before.reshape(-1, 128)], axis=0)
-    before = moved(to_upper, "group", 1)
-    after = moved(to_lower, "group", -1)
-
+        name="front",
+    )(
+        active,
+        active.reshape(1, LEAF_DEV),
+        far_list,
+        near_list,
+        pair_list,
+        jnp.asarray(moment_rows()),
+        jnp.asarray(spreading()),
+        positions,
+        strengths,
+        m2l_ops,
+    )
+
+    lower = moved(to_upper, "dev", 1)
+    upper = moved(to_lower, "dev", -1)
+    cost = pl.CostEstimate(flops=4_000_000_000, bytes_accessed=4_000_000, transcendentals=0)
     total_shape = jax.ShapeDtypeStruct((ACT_MOST + 1, 8, LEAF_PART), F32)
     total = pl.pallas_call(
         self_kernel,
         out_shape=total_shape,
-        in_specs=[SMEM, SMEM, VMEM, VMEM],
+        in_specs=[SMEM, SMEM, VMEM],
         out_specs=VMEM,
-        compiler_params=params,
-        cost_estimate=pl.CostEstimate(flops=4_000_000_000, bytes_accessed=4_000_000, transcendentals=0),
+        scratch_shapes=[shifts],
+        compiler_params=small,
+        cost_estimate=cost,
         name="self_pairs",
-    )(lists, index, packet, shifts)
-    before, after, total = lax.optimization_barrier((before, after, total))
-
-    rows = 3 * ACT_MOST
-
-    def summed(step):
-        base = 3 * PACKET + step * rows
-        return blocks[step] + before[base : base + rows] + after[base : base + rows]
-
-    from_lower = moved(summed(2), "dev", 1)
-    from_upper = moved(summed(0), "dev", -1)
+    )(lists, index, to_upper)
+    lower, upper, total = lax.optimization_barrier((lower, upper, total))
+
+    relayed = jax.ShapeDtypeStruct((3 * PACKET + ROWS_FAR, 128), F32)
+    to_after, to_before = pl.pallas_call(
+        relay_kernel,
+        out_shape=(relayed, relayed),
+        in_specs=[VMEM] * 4,
+        out_specs=(VMEM, VMEM),
+        compiler_params=small,
+        name="relay",
+    )(lower, to_upper, upper, stay)
+    before = moved(to_after, "group", 1)
+    after = moved(to_before, "group", -1)
 
     total = pl.pallas_call(
         local_kernel,
         out_shape=total_shape,
-        in_specs=[SMEM, SMEM, VMEM, VMEM, VMEM],
+        in_specs=[SMEM, SMEM, VMEM, VMEM],
         out_specs=VMEM,
-        compiler_params=params,
-        cost_estimate=pl.CostEstimate(flops=4_000_000_000, bytes_accessed=4_000_000, transcendentals=0),
+        scratch_shapes=[shifts],
+        compiler_params=small,
+        cost_estimate=cost,
         name="local_pairs",
-    )(lists, index, packet, shifts, total)
-    from_lower, from_upper, total = lax.optimization_barrier((from_lower, from_upper, total))
+    )(lists, index, to_upper, total)
+    before, after, total = lax.optimization_barrier((before, after, total))
 
     return pl.pallas_call(
         remote_kernel,
         out_shape=jax.ShapeDtypeStruct(positions.shape, F32),
-        in_specs=[SMEM, SMEM]
-        + [VMEM] * 11,
+        in_specs=[SMEM, SMEM] + [VMEM] * 8,
         out_specs=VMEM,
         scratch_shapes=[
             pltpu.VMEM((ACT_MOST + 1, 8, LEAF_PART), F32),
-            pltpu.VMEM((rows, COEF), F32),
+            pltpu.VMEM((ROWS_FAR, COEF), F32),
+            shifts,
             pltpu.VMEM((32, 128), jnp.int32),
             pltpu.SMEM((32, 128), jnp.int32),
             pltpu.SemaphoreType.DMA,
         ],
-        compiler_params=params,
-        cost_estimate=pl.CostEstimate(flops=4_000_000_000, bytes_accessed=4_000_000, transcendentals=0),
+        compiler_params=small,
+        cost_estimate=cost,
         name="remote_pairs",
-    )(
-        lists,
-        index,
-        packet,
-        shifts,
-        total,
-        before,
-        after,
-        lower,
-        upper,
-        blocks,
-        from_lower,
-        from_upper,
-        jnp.asarray(basis_rows()),
-    )
+    )(lists, index, to_upper, total, before, after, lower, upper, stay, jnp.asarray(basis_rows()))
 
 
 def solution(mesh):

time: 70.3 us -> 52.8 us (0.75)
  the two profiles are of different devices: /device:TPU:260 before, /device:TPU:449 now
where the time goes in v2:
time: 52.8 us; the launch traced here: 52.4 us
  Pallas kernels  31.7 us (60%)
  starting transfers between devices  13.9 us (26%)
  waiting for transfers between devices  5.15 us (10%)
  local copies, waits for them, and re-layouts  1.61 us (3%)
    ppermute x4, starting transfers between devices, moved(): lax.ppermute(value, axis, [(source, source + step) for source in range(fi...  13.9 us
    pallas_call x1, Pallas kernels, on_device(): pl.pallas_call(remote_kernel, out_shape=jax.ShapeDtypeStruct(positions.sh...  11.8 us
    pallas_call x1, Pallas kernels, on_device(): pl.pallas_call(front_kernel, out_shape=(message, message, jax.ShapeDtypeS...  10.9 us
    pallas_call x1, Pallas kernels, on_device(): pl.pallas_call(self_kernel, out_shape=total_shape, in_specs=[SMEM, SMEM,...  5.52 us
    ppermute x4, waiting for transfers between devices, moved(): lax.ppermute(value, axis, [(source, source + step) for source in range(fi...  5.15 us
    pallas_call x1, Pallas kernels, on_device(): pl.pallas_call(local_kernel, out_shape=total_shape, in_specs=[SMEM, SMEM,...  3.36 us
    unnamed x10, local copies, waits for them, and re-layouts  1.61 us
  transfers between devices with their start and end apart: 4, of which 2 were waited for; matrix products, arithmetic and copies ran while one was open for 0% of the time, Pallas kernels for 17%

profile of v2, /device:TPU:449, one launch (start us, length us, event | category | flops | bytes accessed | tf_op | source)
XLA Modules:
  0.0 52.4 jit_solution(14521048792657404788)
XLA Ops:
  0.0 10.9 %front.1 = (f32[488,128]{1,0:T(8,128)}, f32[488,128]{1,0:T(8,128)}, f32[3,96,128]{2,1,0:T(8,128)}, s32[8,128]{1,0:T(8,128)}, s32[64]{0:T(128)}) custom-call(s32[256]{0:T(256)} %flags_ref.1, s32[1,256]{1,0:T(1,128)} %bitcast.5, s32[3,1,1152]{2,1,0:T(1,128)} %bitcast.4, s32[3,1,128]{2,1,0:T(1,128)} %bitcast.6, s32[3,1,128]{2,1,0:T(1,128)} %bitcast.7, ...), custom_call_target="tpu_custom_call" | custom-call | tf_op jit(solution)/shard_map/front/pallas_call | solution.py:535
  10.9 0.0 copy-start.2
  10.9 5.1 %collective-permute-start.1 = (f32[488,128]{1,0:T(8,128)}, f32[488,128]{1,0:T(8,128)S(1)}, u32[]{:S(2)}, u32[]{:S(2)}) collective-permute-start(f32[488,128]{1,0:T(8,128)} %get-tuple-element.21), channel_id=1, source_target_pairs={{1,0},{2,1},{3,2},{4,3},{5,4},{6,5},{7,6},{8,7},{9,8},{10,9},{11,1... | collective-permute-start | bytes 749576 | tf_op jit(solution)/shard_map/ppermute | solution.py:517
  16.0 1.9 %collective-permute-start = (f32[488,128]{1,0:T(8,128)}, f32[488,128]{1,0:T(8,128)S(1)}, u32[]{:S(2)}, u32[]{:S(2)}) collective-permute-start(f32[488,128]{1,0:T(8,128)} %get-tuple-element.20.packet_ref.own_ref), channel_id=1, source_target_pairs={{0,1},{1,2},{2,3},{3,4},{4,5},{5,6},{6,7},{7,8},{8,9},{9,10},{10,1... | collective-permute-start | bytes 749576 | tf_op jit(solution)/shard_map/ppermute | solution.py:517
  18.0 0.0 copy-start.3
  18.0 0.0 copy-done.2
  18.0 0.6 %copy-done.3 = s32[64]{0:T(128)S(1)} copy-done((s32[64]{0:T(128)S(1)}, s32[64]{0:T(128)}, u32[]{:S(2)}) %copy-start.3) | copy-done | bytes 280
  18.6 0.0 copy-start
  18.6 0.9 %copy-done = f32[488,128]{1,0:T(8,128)S(1)} copy-done((f32[488,128]{1,0:T(8,128)S(1)}, f32[488,128]{1,0:T(8,128)}, u32[]{:S(2)}) %copy-start) | copy-done | bytes 249880
  19.6 0.0 copy-start.1
  19.6 5.5 %self_pairs.1.near_ref = f32[33,8,128]{2,1,0:T(8,128)S(1)} custom-call(s32[8,128]{1,0:T(8,128)S(1)} %copy-done.2, s32[64]{0:T(128)S(1)} %copy-done.3, f32[488,128]{1,0:T(8,128)S(1)} %copy-done), custom_call_target="tpu_custom_call" | custom-call | flops 4000000000 | bytes 4000000 | tf_op jit(solution)/shard_map/self_pairs/pallas_call | solution.py:582
  25.1 0.0 collective-permute-done.1.upper_ref
  25.1 1.7 %collective-permute-done.lower_ref = f32[488,128]{1,0:T(8,128)S(1)} collective-permute-done((f32[488,128]{1,0:T(8,128)}, f32[488,128]{1,0:T(8,128)S(1)}, u32[]{:S(2)}, u32[]{:S(2)}) %collective-permute-start) | collective-permute-done | bytes 249888 | tf_op jit(solution)/shard_map/ppermute | solution.py:517
  26.8 0.0 copy-done.1
  26.9 4.9 %collective-permute-start.2 = (f32[696,128]{1,0:T(8,128)S(1)}, f32[696,128]{1,0:T(8,128)S(1)}, u32[]{:S(2)}, u32[]{:S(2)}) collective-permute-start(f32[696,128]{1,0:T(8,128)S(1)} %get-tuple-element.25), channel_id=1, source_target_pairs={{0,64},{64,128},{128,192},{192,256},{256,320},{320,384},{384,448},... | collective-permute-start | bytes 1069064 | tf_op jit(solution)/shard_map/ppermute | solution.py:517
  31.8 0.0 copy-start.4
  31.8 2.1 %collective-permute-start.3 = (f32[696,128]{1,0:T(8,128)S(1)}, f32[696,128]{1,0:T(8,128)S(1)}, u32[]{:S(2)}, u32[]{:S(2)}) collective-permute-start(f32[696,128]{1,0:T(8,128)S(1)} %get-tuple-element.26), channel_id=1, source_target_pairs={{64,0},{128,64},{192,128},{256,192},{320,256},{384,320},{448,384},... | collective-permute-start | bytes 1069064 | tf_op jit(solution)/shard_map/ppermute | solution.py:517
  33.8 3.4 %local_pairs.1.near_ref = f32[33,8,128]{2,1,0:T(8,128)S(1)} custom-call(s32[8,128]{1,0:T(8,128)S(1)} %copy-done.2, s32[64]{0:T(128)S(1)} %copy-done.3, f32[488,128]{1,0:T(8,128)S(1)} %copy-done, f32[33,8,128]{2,1,0:T(8,128)S(1)} %self_pairs.1.near_ref), custom_call_target="tpu_custom_call" | custom-call | flops 4000000000 | bytes 4000000 | tf_op jit(solution)/shard_map/local_pairs/pallas_call | solution.py:606
  37.2 0.0 collective-permute-done.2.before_ref
  37.2 3.4 %collective-permute-done.3.after_ref = f32[696,128]{1,0:T(8,128)S(1)} collective-permute-done((f32[696,128]{1,0:T(8,128)S(1)}, f32[696,128]{1,0:T(8,128)S(1)}, u32[]{:S(2)}, u32[]{:S(2)}) %collective-permute-start.3) | collective-permute-done | bytes 356384 | tf_op jit(solution)/shard_map/ppermute | solution.py:517
  40.6 0.0 copy-done.4
  40.6 11.8 %remote_pairs.1 = f32[3,32768]{1,0:T(4,128)} custom-call(s32[8,128]{1,0:T(8,128)S(1)} %copy-done.2, s32[64]{0:T(128)S(1)} %copy-done.3, f32[488,128]{1,0:T(8,128)S(1)} %copy-done, f32[33,8,128]{2,1,0:T(8,128)S(1)} %local_pairs.1.near_ref, f32[696,128]{1,0:T(8,128)S(1)} %collective-permute-done.2.before_ref, f32[696,128]{1,0:T(8,128)S(1)} %collective-permute-done.3.after_ref, ...), custom_call_target="tpu_custom_call" | custom-call | flops 4000000000 | bytes 4000000 | tf_op jit(solution)/shard_map/remote_pairs/pallas_call | solution.py:618
  (1 shorter events, 0.0 us)
Async XLA Ops:
  10.9 7.0 %copy-start.2 = (s32[8,128]{1,0:T(8,128)S(1)}, s32[8,128]{1,0:T(8,128)}, u32[]{:S(2)}) copy-start(s32[8,128]{1,0:T(8,128)} %get-tuple-element.18.lists_ref) | copy-start | bytes 12292
  10.9 14.2 %collective-permute-start.1 = (f32[488,128]{1,0:T(8,128)}, f32[488,128]{1,0:T(8,128)S(1)}, u32[]{:S(2)}, u32[]{:S(2)}) collective-permute-start(f32[488,128]{1,0:T(8,128)} %get-tuple-element.21), channel_id=1, source_target_pairs={{1,0},{2,1},{3,2},{4,3},{5,4},{6,5},{7,6},{8,7},{9,8},{10,9},{11,1... | collective-permute-start | bytes 749576 | tf_op jit(solution)/shard_map/ppermute | solution.py:517
  16.0 10.8 %collective-permute-start = (f32[488,128]{1,0:T(8,128)}, f32[488,128]{1,0:T(8,128)S(1)}, u32[]{:S(2)}, u32[]{:S(2)}) collective-permute-start(f32[488,128]{1,0:T(8,128)} %get-tuple-element.20.packet_ref.own_ref), channel_id=1, source_target_pairs={{0,1},{1,2},{2,3},{3,4},{4,5},{5,6},{6,7},{7,8},{8,9},{9,10},{10,1... | collective-permute-start | bytes 749576 | tf_op jit(solution)/shard_map/ppermute | solution.py:517
  18.0 0.7 %copy-start.3 = (s32[64]{0:T(128)S(1)}, s32[64]{0:T(128)}, u32[]{:S(2)}) copy-start(s32[64]{0:T(128)} %get-tuple-element.19.index_ref) | copy-start | bytes 772
  18.6 0.9 %copy-start = (f32[488,128]{1,0:T(8,128)S(1)}, f32[488,128]{1,0:T(8,128)}, u32[]{:S(2)}) copy-start(f32[488,128]{1,0:T(8,128)} %get-tuple-element.20.packet_ref.own_ref) | copy-start | bytes 749572
  19.6 7.3 %copy-start.1 = (f32[3,96,128]{2,1,0:T(8,128)S(1)}, f32[3,96,128]{2,1,0:T(8,128)}, u32[]{:S(2)}) copy-start(f32[3,96,128]{2,1,0:T(8,128)} %get-tuple-element.24.stay_ref) | copy-start | bytes 442372
  26.9 10.3 %collective-permute-start.2 = (f32[696,128]{1,0:T(8,128)S(1)}, f32[696,128]{1,0:T(8,128)S(1)}, u32[]{:S(2)}, u32[]{:S(2)}) collective-permute-start(f32[696,128]{1,0:T(8,128)S(1)} %get-tuple-element.25), channel_id=1, source_target_pairs={{0,64},{64,128},{128,192},{192,256},{256,320},{320,384},{384,448},... | collective-permute-start | bytes 1069064 | tf_op jit(solution)/shard_map/ppermute | solution.py:517
  31.8 8.8 %copy-start.4 = (bf16[384,96]{1,0:T(8,128)(2,1)S(1)}, bf16[384,96]{1,0:T(8,128)(2,1)}, u32[]{:S(2)}) copy-start(bf16[384,96]{1,0:T(8,128)(2,1)} %constant.8.clone.mix_ref) | copy-start | bytes 221188
  31.8 8.8 %collective-permute-start.3 = (f32[696,128]{1,0:T(8,128)S(1)}, f32[696,128]{1,0:T(8,128)S(1)}, u32[]{:S(2)}, u32[]{:S(2)}) collective-permute-start(f32[696,128]{1,0:T(8,128)S(1)} %get-tuple-element.26), channel_id=1, source_target_pairs={{64,0},{128,64},{192,128},{256,192},{320,256},{384,320},{448,384},... | collective-permute-start | bytes 1069064 | tf_op jit(solution)/shard_map/ppermute | solution.py:517

commit v3 on v2

--- a/solution.py
+++ b/solution.py
@@ -22,8 +22,10 @@
 PACKET = META + 8
 ROWS_FAR = 3 * ACT_MOST
 GROUP_LEAVES = 8
-PAIRS = 16
-FIRST = 4
+CHUNKS = 2
+PAIRS = 32
+SIDE = 16
+FIRST = 1
 SMOOTH = 0.04
 FORWARD_GROUP = (-1, -1, -1, 0)
 FORWARD_MEMBER = (-1, 0, 1, -1)
@@ -153,12 +155,22 @@
     pairs_ref,
     sems,
 ):
-    copies = [
-        pltpu.make_async_copy(pos_hbm, pos_ref, sems.at[0]),
-        pltpu.make_async_copy(str_hbm, str_ref, sems.at[1]),
-        pltpu.make_async_copy(ops_hbm, ops_ref, sems.at[2]),
+    span = pos_ref.shape[1] // CHUNKS
+
+    def arriving(chunk):
+        here = pl.ds(pl.multiple_of(chunk * span, span), span)
+        return [
+            pltpu.make_async_copy(pos_hbm.at[:, here], pos_ref.at[:, here], sems.at[chunk]),
+            pltpu.make_async_copy(str_hbm.at[:, here], str_ref.at[:, here], sems.at[CHUNKS + chunk]),
+        ]
+
+    operators = [
+        pltpu.make_async_copy(
+            ops_hbm.at[part * 8 : part * 8 + 8], ops_ref.at[part * 8 : part * 8 + 8], sems.at[2 * CHUNKS + part]
+        )
+        for part in range(OFFSETS // 8)
     ]
-    for copy in copies:
+    for copy in [copy for chunk in range(CHUNKS) for copy in arriving(chunk)] + operators:
         copy.start()
     for flat, ref, blocks in ((far_flat, far_ref, 9), (near_flat, near_ref, 1), (pairs_flat, pairs_ref, 1)):
         for kind in range(3):
@@ -222,20 +234,6 @@
         place_ref[rows, :] = (iota((128, 128), 0) == key).astype(F32).astype(BF16)
         pick_ref[rows, :] = (sources[:, direction : direction + 1] == leaves).astype(F32).astype(BF16)
 
-    copies[0].wait()
-    copies[1].wait()
-    for ref in (to_upper_ref, to_lower_ref):
-        ref[META : META + 1, :] = first_slot.astype(F32)
-        ref[META + 1 : META + 2, :] = second_slot.astype(F32)
-        ref[META + 2 : META + 3, :] = codes.astype(F32)
-        ref[META + 3 : PACKET, :] = jnp.zeros((5, 128), F32)
-    for slot in range(ACT_MOST):
-        leaf = jnp.where(slot < count, index_ref[slot], 0)
-        here = pl.ds(pl.multiple_of(leaf * LEAF_PART, LEAF_PART), LEAF_PART)
-        for ref in (to_upper_ref, to_lower_ref):
-            ref[ROWS_LEAF * slot : ROWS_LEAF * slot + 3, :] = pos_ref[:, here]
-            ref[ROWS_LEAF * slot + 3 : ROWS_LEAF * slot + 6, :] = str_ref[:, here]
-
     mix = mix_ref[...]
     width = GROUP_LEAVES * LEAF_PART
     lane_leaf = iota((32, 128), 1) // 16
@@ -272,8 +270,29 @@
         cell_ref[pl.ds(pl.multiple_of(block * 128, 128), 128), :] = cells.T
         return carry
 
-    lax.fori_loop(0, LEAF_DEV // GROUP_LEAVES, expand, 0, unroll=8)
-    lax.fori_loop(0, LEAF_DEV // GROUP_LEAVES, contract, 0, unroll=8)
+    blocks = LEAF_DEV // GROUP_LEAVES // CHUNKS
+
+    def expand_chunk(chunk, carry):
+        for copy in arriving(chunk):
+            copy.wait()
+        for block in range(blocks):
+            expand(chunk * blocks + block, carry)
+        return carry
+
+    lax.fori_loop(0, CHUNKS, expand_chunk, 0)
+    for ref in (to_upper_ref, to_lower_ref):
+        ref[META : META + 1, :] = first_slot.astype(F32)
+        ref[META + 1 : META + 2, :] = second_slot.astype(F32)
+        ref[META + 2 : META + 3, :] = codes.astype(F32)
+        ref[META + 3 : PACKET, :] = jnp.zeros((5, 128), F32)
+    for slot in range(ACT_MOST):
+        leaf = jnp.where(slot < count, index_ref[slot], 0)
+        here = pl.ds(pl.multiple_of(leaf * LEAF_PART, LEAF_PART), LEAF_PART)
+        for ref in (to_upper_ref, to_lower_ref):
+            ref[ROWS_LEAF * slot : ROWS_LEAF * slot + 3, :] = pos_ref[:, here]
+            ref[ROWS_LEAF * slot + 3 : ROWS_LEAF * slot + 6, :] = str_ref[:, here]
+
+    lax.fori_loop(0, LEAF_DEV // GROUP_LEAVES, contract, 0, unroll=16)
     for c in range(3):
         total = jnp.zeros((LEAF_DEV, COEF), F32)
         for a in range(ORDER):
@@ -281,7 +300,8 @@
             total = total + dot(piece, spread_ref[a])
         moment_ref[:, c * COEF : (c + 1) * COEF] = total.astype(BF16)
 
-    copies[2].wait()
+    for copy in operators:
+        copy.wait()
     got_ref[...] = dot(pick_ref[...], moment_ref[...]).astype(BF16)
     for direction in range(9):
         residue = 8 - direction
@@ -321,7 +341,7 @@
         row < 3, high, jnp.where(row == 3, norm_high, jnp.where(row == 4, norm_mid, jnp.where(row == 5, norm_low, 1.0)))
     )
     second = jnp.where(row == 3, 1.0, low)
-    return jnp.concatenate([first, second, high, low], axis=0).T.astype(BF16)
+    return jnp.concatenate([first, second, high, low], axis=0)
 
 
 def target_features(raw, shift):
@@ -353,30 +373,38 @@
     return packet_ref[pl.ds(base + slot * ROWS_LEAF, 8), :]
 
 
-def effect(target, source, shift):
-    kernel = lax.rsqrt(dot(source_features(source), target_features(target, shift)))
-    rows = source_rows(source)
-    return dot(jnp.concatenate([rows, rows], axis=1), jnp.concatenate(split(kernel), axis=0))
-
-
-def self_kernel(lists_ref, index_ref, packet_ref, total_ref, shift_ref):
+def effects(parts):
+    results = []
+    nothing = jnp.zeros((32, LEAF_PART), BF16)
+    for at in range(0, len(parts), 2):
+        (target, source, shift), (target_too, source_too, shift_too) = parts[at : at + 2]
+        sources = jnp.concatenate([source_features(source), source_features(source_too)], axis=0).T.astype(BF16)
+        targets = jnp.concatenate(
+            [
+                jnp.concatenate([target_features(target, shift), nothing], axis=1),
+                jnp.concatenate([nothing, target_features(target_too, shift_too)], axis=1),
+            ],
+            axis=0,
+        )
+        kernel = jnp.concatenate(split(lax.rsqrt(dot(sources, targets))), axis=0)
+        rows = jnp.concatenate([source_rows(source), source_rows(source_too)], axis=0)
+        terms = dot(jnp.concatenate([rows, rows], axis=1), kernel)
+        results += [terms[0:8, 0:LEAF_PART], terms[8:16, LEAF_PART:]]
+    return results
+
+
+def self_kernel(lists_ref, index_ref, message_hbm, total_ref, packet_ref, shift_ref, sem):
+    copy = pltpu.make_async_copy(message_hbm.at[0:PACKET], packet_ref, sem)
+    copy.start()
     displacements(shift_ref)
     total_ref[...] = jnp.zeros_like(total_ref)
-    count = index_ref[ACT_MOST]
     still = jnp.zeros((8, LEAF_PART), F32)
-    group = 16
-
-    def alone(step, carry):
-        results = []
-        for at in range(group):
-            raw = leaf_rows(packet_ref, step * group + at)
-            results.append(effect(raw, raw, still))
-        for at in range(group):
-            total_ref[step * group + at] = results[at]
-        return carry
-
-    lax.fori_loop(0, pl.cdiv(count, group), alone, 0)
-    local_pairs(lists_ref, packet_ref, shift_ref, total_ref, 0, jnp.minimum(pl.cdiv(4 * count, PAIRS), FIRST))
+    copy.wait()
+    raws = [leaf_rows(packet_ref, slot) for slot in range(ACT_MOST)]
+    for slot, terms in enumerate(effects([(raw, raw, still) for raw in raws])):
+        total_ref[slot] = terms
+    end = jnp.minimum(pl.cdiv(4 * index_ref[ACT_MOST], PAIRS), FIRST)
+    local_pairs(lists_ref, packet_ref, shift_ref, total_ref, 0, end)
 
 
 def local_kernel(lists_ref, index_ref, packet_ref, near_ref, total_ref, shift_ref):
@@ -387,7 +415,7 @@
 
 def local_pairs(lists_ref, packet_ref, shift_ref, total_ref, begin, end):
     def pairs(step, carry):
-        results = []
+        slots, parts = [], []
         for at in range(PAIRS):
             column = step * PAIRS + at
             first = lists_ref[0, column]
@@ -395,9 +423,9 @@
             code = lists_ref[2, column]
             one = leaf_rows(packet_ref, first)
             other = leaf_rows(packet_ref, second)
-            results.append((first, effect(one, other, shift_ref[32 + code])))
-            results.append((second, effect(other, one, shift_ref[code])))
-        for slot, terms in results:
+            slots += [first, second]
+            parts += [(one, other, shift_ref[32 + code]), (other, one, shift_ref[code])]
+        for slot, terms in zip(slots, effects(parts)):
             total_ref[slot] += terms
         return carry
 
@@ -449,8 +477,8 @@
         def columns(step, carry):
             picks = []
             for side, (ref, place) in enumerate(sides):
-                for at in range(PCAP // 4):
-                    picks.append((side, ref, place, side * PCAP + step * (PCAP // 4) + at))
+                for at in range(SIDE):
+                    picks.append((side, ref, place, side * PCAP + step * SIDE + at))
             targets = [target_of(side, column) for side, ref, place, column in picks]
             live = targets[0] != DEAD
             for target in targets[1:]:
@@ -458,17 +486,17 @@
 
             @pl.when(live)
             def _():
-                results = []
+                parts = []
                 for target, (side, ref, place, column) in zip(targets, picks):
                     source = leaf_rows(ref, source_of(side, column), place * PACKET)
                     shift = shift_ref[sign + code_of(side, column)]
-                    results.append(effect(leaf_rows(packet_ref, target), source, shift))
-                for target, terms in zip(targets, results):
+                    parts.append((leaf_rows(packet_ref, target), source, shift))
+                for target, terms in zip(targets, effects(parts)):
                     total_ref[target] += terms
 
             return carry
 
-        lax.fori_loop(0, 4, columns, 0)
+        lax.fori_loop(0, PCAP // SIDE, columns, 0)
 
     all_sides(front, lambda side, c: lists_ref[3, c], lambda side, c: lists_ref[4, c], lambda side, c: lists_ref[5, c], 32)
     copy.wait()
@@ -558,7 +586,7 @@
             pltpu.VMEM((32, 128), jnp.int32),
             pltpu.VMEM((8, 128), jnp.int32),
             pltpu.VMEM((8, 128), jnp.int32),
-            pltpu.SemaphoreType.DMA((3,)),
+            pltpu.SemaphoreType.DMA((2 * CHUNKS + OFFSETS // 8,)),
         ],
         compiler_params=params,
         name="front",
@@ -582,10 +610,10 @@
     total = pl.pallas_call(
         self_kernel,
         out_shape=total_shape,
-        in_specs=[SMEM, SMEM, VMEM],
+        in_specs=[SMEM, SMEM, HBM],
         out_specs=VMEM,
-        scratch_shapes=[shifts],
-        compiler_params=small,
+        scratch_shapes=[pltpu.VMEM((PACKET, 128), F32), shifts, pltpu.SemaphoreType.DMA],
+        compiler_params=params,
         cost_estimate=cost,
         name="self_pairs",
     )(lists, index, to_upper)

time: 52.8 us -> 49 us (0.928)
  the two profiles are of different devices: /device:TPU:449 before, /device:TPU:69 now
where the time goes in v3:
time: 49 us; the launch traced here: 48.7 us
  Pallas kernels  28.7 us (59%)
  starting transfers between devices  12.7 us (26%)
  waiting for transfers between devices  7.01 us (14%)
    ppermute x4, starting transfers between devices, moved(): lax.ppermute(value, axis, [(source, source + step) for source in range(fi...  12.7 us
    pallas_call x1, Pallas kernels, on_device(): pl.pallas_call(remote_kernel, out_shape=jax.ShapeDtypeStruct(positions.sh...  10.1 us
    pallas_call x1, Pallas kernels, on_device(): pl.pallas_call(front_kernel, out_shape=(message, message, jax.ShapeDtypeS...  9.98 us
    ppermute x4, waiting for transfers between devices, moved(): lax.ppermute(value, axis, [(source, source + step) for source in range(fi...  7.01 us
    pallas_call x1, Pallas kernels, on_device(): pl.pallas_call(self_kernel, out_shape=total_shape, in_specs=[SMEM, SMEM,...  4.8 us
    pallas_call x1, Pallas kernels, on_device(): pl.pallas_call(local_kernel, out_shape=total_shape, in_specs=[SMEM, SMEM,...  3.75 us
  transfers between devices with their start and end apart: 4, of which 2 were waited for; matrix products, arithmetic and copies ran while one was open for 0% of the time, Pallas kernels for 18%

profile of v3, /device:TPU:69, one launch (start us, length us, event | category | flops | bytes accessed | tf_op | source)
XLA Modules:
  0.0 48.7 jit_solution(17297463374149874903)
XLA Ops:
  0.0 10.0 %front.1 = (f32[488,128]{1,0:T(8,128)}, f32[488,128]{1,0:T(8,128)}, f32[3,96,128]{2,1,0:T(8,128)}, s32[8,128]{1,0:T(8,128)}, s32[64]{0:T(128)}) custom-call(s32[256]{0:T(256)} %flags_ref.1, s32[1,256]{1,0:T(1,128)} %bitcast.5, s32[3,1,1152]{2,1,0:T(1,128)} %bitcast.4, s32[3,1,128]{2,1,0:T(1,128)} %bitcast.6, s32[3,1,128]{2,1,0:T(1,128)} %bitcast.7, ...), custom_call_target="tpu_custom_call" | custom-call | tf_op jit(solution)/shard_map/front/pallas_call | solution.py:563
  10.0 4.2 %collective-permute-start.1 = (f32[488,128]{1,0:T(8,128)}, f32[488,128]{1,0:T(8,128)S(1)}, u32[]{:S(2)}, u32[]{:S(2)}) collective-permute-start(f32[488,128]{1,0:T(8,128)} %get-tuple-element.21), channel_id=1, source_target_pairs={{1,0},{2,1},{3,2},{4,3},{5,4},{6,5},{7,6},{8,7},{9,8},{10,9},{11,1... | collective-permute-start | bytes 749576 | tf_op jit(solution)/shard_map/ppermute | solution.py:545
  14.2 1.9 %collective-permute-start = (f32[488,128]{1,0:T(8,128)}, f32[488,128]{1,0:T(8,128)S(1)}, u32[]{:S(2)}, u32[]{:S(2)}) collective-permute-start(f32[488,128]{1,0:T(8,128)} %get-tuple-element.20.message_hbm.own_ref.packet_ref), channel_id=1, source_target_pairs={{0,1},{1,2},{2,3},{3,4},{4,5},{5,6},{6,7},{7,8},{8,9},{9,10},{10,1... | collective-permute-start | bytes 749576 | tf_op jit(solution)/shard_map/ppermute | solution.py:545
  16.1 0.0 copy-start
  16.1 0.0 copy-start.1
  16.1 4.8 %self_pairs.1.near_ref = f32[33,8,128]{2,1,0:T(8,128)} custom-call(s32[8,128]{1,0:T(8,128)} %get-tuple-element.18.lists_ref, s32[64]{0:T(128)} %get-tuple-element.19.index_ref, f32[488,128]{1,0:T(8,128)} %get-tuple-element.20.message_hbm.own_ref.packet_ref), custom_call_target="tpu_custom_call" | custom-call | flops 4000000000 | bytes 4000000 | tf_op jit(solution)/shard_map/self_pairs/pallas_call | solution.py:610
  21.0 0.0 collective-permute-done.1.upper_ref
  21.0 4.0 %collective-permute-done.lower_ref = f32[488,128]{1,0:T(8,128)S(1)} collective-permute-done((f32[488,128]{1,0:T(8,128)}, f32[488,128]{1,0:T(8,128)S(1)}, u32[]{:S(2)}, u32[]{:S(2)}) %collective-permute-start) | collective-permute-done | bytes 249888 | tf_op jit(solution)/shard_map/ppermute | solution.py:545
  25.0 0.0 copy-done
  25.0 0.0 copy-done.1
  25.0 0.0 copy-start.2
  25.0 0.1 relay.1
  25.1 0.0 copy-start.3
  25.1 4.6 %collective-permute-start.2 = (f32[696,128]{1,0:T(8,128)S(1)}, f32[696,128]{1,0:T(8,128)S(1)}, u32[]{:S(2)}, u32[]{:S(2)}) collective-permute-start(f32[696,128]{1,0:T(8,128)S(1)} %get-tuple-element.25), channel_id=1, source_target_pairs={{0,64},{64,128},{128,192},{192,256},{256,320},{320,384},{384,448},... | collective-permute-start | bytes 1069064 | tf_op jit(solution)/shard_map/ppermute | solution.py:545
  29.7 0.0 copy-start.4
  29.7 2.1 %collective-permute-start.3 = (f32[696,128]{1,0:T(8,128)S(1)}, f32[696,128]{1,0:T(8,128)S(1)}, u32[]{:S(2)}, u32[]{:S(2)}) collective-permute-start(f32[696,128]{1,0:T(8,128)S(1)} %get-tuple-element.26), channel_id=1, source_target_pairs={{64,0},{128,64},{192,128},{256,192},{320,256},{384,320},{448,384},... | collective-permute-start | bytes 1069064 | tf_op jit(solution)/shard_map/ppermute | solution.py:545
  31.7 0.0 copy-done.2
  31.7 0.0 copy-done.5
  31.8 0.0 copy-done.3
  31.8 3.8 %local_pairs.1.near_ref = f32[33,8,128]{2,1,0:T(8,128)S(1)} custom-call(s32[8,128]{1,0:T(8,128)S(1)} %copy-done.2, s32[64]{0:T(128)S(1)} %copy-done.3, f32[488,128]{1,0:T(8,128)S(1)} %copy-done, f32[33,8,128]{2,1,0:T(8,128)S(1)} %copy-done.5), custom_call_target="tpu_custom_call" | custom-call | flops 4000000000 | bytes 4000000 | tf_op jit(solution)/shard_map/local_pairs/pallas_call | solution.py:634
  35.5 0.0 collective-permute-done.2.before_ref
  35.5 3.0 %collective-permute-done.3.after_ref = f32[696,128]{1,0:T(8,128)S(1)} collective-permute-done((f32[696,128]{1,0:T(8,128)S(1)}, f32[696,128]{1,0:T(8,128)S(1)}, u32[]{:S(2)}, u32[]{:S(2)}) %collective-permute-start.3) | collective-permute-done | bytes 356384 | tf_op jit(solution)/shard_map/ppermute | solution.py:545
  38.5 0.0 copy-done.4
  38.5 10.1 %remote_pairs.1 = f32[3,32768]{1,0:T(4,128)} custom-call(s32[8,128]{1,0:T(8,128)S(1)} %copy-done.2, s32[64]{0:T(128)S(1)} %copy-done.3, f32[488,128]{1,0:T(8,128)S(1)} %copy-done, f32[33,8,128]{2,1,0:T(8,128)S(1)} %local_pairs.1.near_ref, f32[696,128]{1,0:T(8,128)S(1)} %collective-permute-done.2.before_ref, f32[696,128]{1,0:T(8,128)S(1)} %collective-permute-done.3.after_ref, ...), custom_call_target="tpu_custom_call" | custom-call | flops 4000000000 | bytes 4000000 | tf_op jit(solution)/shard_map/remote_pairs/pallas_call | solution.py:646
  (1 shorter events, 0.0 us)
Async XLA Ops:
  10.0 11.0 %collective-permute-start.1 = (f32[488,128]{1,0:T(8,128)}, f32[488,128]{1,0:T(8,128)S(1)}, u32[]{:S(2)}, u32[]{:S(2)}) collective-permute-start(f32[488,128]{1,0:T(8,128)} %get-tuple-element.21), channel_id=1, source_target_pairs={{1,0},{2,1},{3,2},{4,3},{5,4},{6,5},{7,6},{8,7},{9,8},{10,9},{11,1... | collective-permute-start | bytes 749576 | tf_op jit(solution)/shard_map/ppermute | solution.py:545
  14.2 10.8 %collective-permute-start = (f32[488,128]{1,0:T(8,128)}, f32[488,128]{1,0:T(8,128)S(1)}, u32[]{:S(2)}, u32[]{:S(2)}) collective-permute-start(f32[488,128]{1,0:T(8,128)} %get-tuple-element.20.message_hbm.own_ref.packet_ref), channel_id=1, source_target_pairs={{0,1},{1,2},{2,3},{3,4},{4,5},{5,6},{6,7},{7,8},{8,9},{9,10},{10,1... | collective-permute-start | bytes 749576 | tf_op jit(solution)/shard_map/ppermute | solution.py:545
  16.1 8.9 %copy-start = (f32[488,128]{1,0:T(8,128)S(1)}, f32[488,128]{1,0:T(8,128)}, u32[]{:S(2)}) copy-start(f32[488,128]{1,0:T(8,128)} %get-tuple-element.20.message_hbm.own_ref.packet_ref) | copy-start | bytes 749572
  16.1 8.9 %copy-start.1 = (f32[3,96,128]{2,1,0:T(8,128)S(1)}, f32[3,96,128]{2,1,0:T(8,128)}, u32[]{:S(2)}) copy-start(f32[3,96,128]{2,1,0:T(8,128)} %get-tuple-element.24.stay_ref) | copy-start | bytes 442372
  25.0 6.7 %copy-start.2 = (s32[8,128]{1,0:T(8,128)S(1)}, s32[8,128]{1,0:T(8,128)}, u32[]{:S(2)}) copy-start(s32[8,128]{1,0:T(8,128)} %get-tuple-element.18.lists_ref) | copy-start | bytes 12292
  25.0 6.7 %copy-start.5 = (f32[33,8,128]{2,1,0:T(8,128)S(1)}, f32[33,8,128]{2,1,0:T(8,128)}, u32[]{:S(2)}) copy-start(f32[33,8,128]{2,1,0:T(8,128)} %self_pairs.1.near_ref) | copy-start | bytes 405508
  25.1 6.7 %copy-start.3 = (s32[64]{0:T(128)S(1)}, s32[64]{0:T(128)}, u32[]{:S(2)}) copy-start(s32[64]{0:T(128)} %get-tuple-element.19.index_ref) | copy-start | bytes 772
  25.1 10.4 %collective-permute-start.2 = (f32[696,128]{1,0:T(8,128)S(1)}, f32[696,128]{1,0:T(8,128)S(1)}, u32[]{:S(2)}, u32[]{:S(2)}) collective-permute-start(f32[696,128]{1,0:T(8,128)S(1)} %get-tuple-element.25), channel_id=1, source_target_pairs={{0,64},{64,128},{128,192},{192,256},{256,320},{320,384},{384,448},... | collective-permute-start | bytes 1069064 | tf_op jit(solution)/shard_map/ppermute | solution.py:545
  29.7 8.8 %copy-start.4 = (bf16[384,96]{1,0:T(8,128)(2,1)S(1)}, bf16[384,96]{1,0:T(8,128)(2,1)}, u32[]{:S(2)}) copy-start(bf16[384,96]{1,0:T(8,128)(2,1)} %constant.8.clone.mix_ref) | copy-start | bytes 221188
  29.7 8.8 %collective-permute-start.3 = (f32[696,128]{1,0:T(8,128)S(1)}, f32[696,128]{1,0:T(8,128)S(1)}, u32[]{:S(2)}, u32[]{:S(2)}) collective-permute-start(f32[696,128]{1,0:T(8,128)S(1)} %get-tuple-element.26), channel_id=1, source_target_pairs={{64,0},{128,64},{192,128},{256,192},{320,256},{384,320},{448,384},... | collective-permute-start | bytes 1069064 | tf_op jit(solution)/shard_map/ppermute | solution.py:545
